TPU v7x, 128 devices: a whole 4x4x4 slice. The times are simulated.
128 devices in a mesh: row: 16 (over x, z_hi, core), col: 8 (over y, z_lo).
Axes of the slice: x: 4, y: 4, z: 4 (z_hi: 2, z_lo: 2; z = z_hi * 2 + z_lo), core: 2. Of those that a mesh axis runs over, the one named last changes fastest.
Arguments:
- skew_matrix: float32 [16384, 16384], P('row', 'col'), may hold values from -80 to 80, as said below
- first_reflector: float32 [16384, 128], P('row'), may hold values from -0.05625 to 0.05625
- first_factor: float32 [128, 128], replicated, may hold values from -0.6 to 1.5, as said below
- second_reflector: float32 [16384, 128], P('row'), may hold values from -0.05625 to 0.05625
- second_factor: float32 [128, 128], replicated, may hold values from -0.6 to 1.5, as said below
- vectors: float32 [16384, 4096], P('row', 'col'), may hold values from -6 to 6
Outputs:
- updated_matrix: float32 [16384, 16384], P('row', 'col')
- back_vectors: float32 [16384, 4096], P('row', 'col')
Inputs may be any that keep to these rules, and one draw needn't show every extreme that they name: skew_matrix is skew-symmetric: entry (i, j) equals minus entry (j, i) exactly. first_factor is upper triangular with a positive diagonal. second_factor is upper triangular with a positive diagonal.
All inputs are finite; a program needn't handle non-finite values.
Results may differ from a plain program's by a relative error of at most 0.000059.
Values sent between devices are 32-bit elements; how exact they have to be, the bound alone decides.
No kernel may reach another device: no remote copies, remote signals or barrier semaphores. Data moves between devices by JAX's collectives and lax.ppermute only.
A program may use at most 128 MiB of HBM per device.

v0:
```python
import jax
import jax.numpy as jnp
from jax import lax
from jax.sharding import PartitionSpec as P


def multiply(left, right):
    return jnp.dot(left, right, precision=lax.Precision.HIGHEST, preferred_element_type=jnp.float32)


def inner_rows(left, right):
    return lax.dot_general(
        left,
        right,
        (((0,), (0,)), ((), ())),
        precision=lax.Precision.HIGHEST,
        preferred_element_type=jnp.float32,
    )


def transform(matrix, own_rows, col_rows, factor):
    partial_rows = multiply(matrix, col_rows)
    summed_rows = lax.psum(partial_rows, "col")
    partial_cols = inner_rows(matrix, own_rows)
    summed_cols = lax.psum(partial_cols, "row")
    plain_cols = -summed_cols
    gram = lax.psum(inner_rows(own_rows, summed_rows), "row")
    correction = multiply(multiply(factor.T, gram), factor)
    fixed_rows = multiply(summed_rows, factor) - 0.5 * multiply(own_rows, correction)
    fixed_cols = multiply(plain_cols, factor) - 0.5 * multiply(col_rows, correction)
    left = jnp.concatenate([own_rows, -fixed_rows], axis=1)
    right = jnp.concatenate([fixed_cols, col_rows], axis=1)
    update = lax.dot_general(
        left,
        right,
        (((1,), (1,)), ((), ())),
        precision=lax.Precision.HIGHEST,
        preferred_element_type=jnp.float32,
    )
    return matrix + update


def shards(skew_matrix, first_reflector, first_factor, second_reflector, second_factor, vectors):
    current = vectors
    for reflector, factor in ((second_reflector, second_factor), (first_reflector, first_factor)):
        sums = lax.psum(inner_rows(reflector, current), "row")
        current = current - multiply(reflector, multiply(factor, sums))
    cols_here = skew_matrix.shape[1]
    col_index = lax.axis_index("col")
    whole_first, whole_second = (
        lax.all_gather(first_reflector, "row", axis=0, tiled=True),
        lax.all_gather(second_reflector, "row", axis=0, tiled=True),
    )
    col_start = col_index * cols_here
    panel_first = lax.dynamic_slice_in_dim(whole_first, col_start, cols_here, 0)
    panel_second = lax.dynamic_slice_in_dim(whole_second, col_start, cols_here, 0)
    inner = transform(skew_matrix, first_reflector, panel_first, first_factor)
    updated_matrix = transform(inner, second_reflector, panel_second, second_factor)
    return (updated_matrix, current)


def solution(mesh):
    in_specs = (P("row", "col"), P("row", None), P(), P("row", None), P(), P("row", "col"))
    out_specs = (P("row", "col"), P("row", "col"))
    return jax.shard_map(shards, mesh=mesh, in_specs=in_specs, out_specs=out_specs, check_vma=False)
```

profile of v0, /device:TPU:1, one launch (start us, length us, event | category | flops | bytes accessed | tf_op | source)
XLA Modules:
  0.0 674.2 jit_solution(10758281256729938577)
XLA Ops:
  8.0 78.8 %all-gather.3.cloned.1.call-done = f32[16384,128]{1,0:T(8,128)} async-done(((f32[1024,128]{1,0:T(8,128)}), f32[16384,128]{1,0:T(8,128)}) %all-gather.3.cloned.1.call-update) | async-done | bytes 8388624 | tf_op jit(solution)/shard_map/all_gather | solution.py:51
  86.8 1.3 constant_dynamic-slice_fusion.1
  88.1 11.9 %convolution_bitcast_fusion = f32[1024,128]{0,1:T(8,128)} fusion(f32[2048,128]{1,0:T(8,128)S(1)} %constant_dynamic-slice_fusion.1, f32[1024,2048]{1,0:T(8,128)} %param.6), kind=kOutput, calls=%fused_computation.14 | convolution fusion | flops 3221225472 | bytes 9961472 | tf_op jit(solution)/shard_map/dot_general | solution.py:8
  101.1 3.7 fusion.35
  104.8 16.4 %fusion.29 = f32[2048,128]{1,0:T(8,128)} fusion(f32[1024,2048]{1,0:T(8,128)} %param.6, f32[1024,128]{1,0:T(8,128)S(1)} %copy-done.3), kind=kOutput, calls=%fused_computation.43 | convolution fusion | flops 3221225472 | bytes 9961472 | tf_op jit(solution)/shard_map/dot_general | solution.py:12
  121.1 45.9 %all-reduce.7.cloned.1.call-done = f32[1024,128]{0,1:T(8,128)} async-done(((f32[1024,128]{0,1:T(8,128)}), f32[1024,128]{0,1:T(8,128)}) %all-reduce.7.cloned.1.call-update) | async-done | bytes 524304 | tf_op jit(solution)/shard_map/psum | solution.py:23
  167.0 2.3 convolution_bitcast_fusion.3
  169.6 2.9 copy.8
  172.5 75.0 %all-gather.5.cloned.1.call-done = f32[16384,128]{1,0:T(8,128)} async-done(((f32[1024,128]{1,0:T(8,128)}), f32[16384,128]{1,0:T(8,128)}) %all-gather.5.cloned.1.call-update) | async-done | bytes 8388624 | tf_op jit(solution)/shard_map/all_gather | solution.py:52
  247.5 1.3 constant_dynamic-slice_fusion
  248.8 3.2 fusion.26
  252.0 138.2 %all-reduce.13.cloned.1.call-done = (f32[2048,128]{1,0:T(8,128)}, f32[128,128]{0,1:T(8,128)}, f32[128,512]{1,0:T(8,128)}) async-done(((f32[2048,128]{1,0:T(8,128)}, f32[128,128]{0,1:T(8,128)}, f32[128,512]{1,0:T(8,128)}), (f32[2048,128]{1,0:T(8,128)}, f32[128,128]{0,1:T(8,128)}, f32[128,512]{1,0:T(8,128)})) %all-reduce.13.cloned.1.call-update) | async-done | bytes 1376272 | tf_op jit(solution)/shard_map/psum | solution.py:25
  390.2 2.2 fusion.22
  394.7 1.6 fusion.13
  396.3 10.1 %convolution_add_fusion.1 = f32[1024,2048]{1,0:T(8,128)S(1)} fusion(f32[1024,2048]{1,0:T(8,128)} %param.6, f32[2048,128]{1,0:T(8,128)S(1)} %constant_dynamic-slice_fusion.1, f32[2048,128]{1,0:T(8,128)S(1)} %fusion.1, f32[1024,128]{1,0:T(8,128)S(1)} %fusion.13, f32[1024,128]{1,0:T(8,128)S(1)} %copy-done.3), kind=kOutput, calls=%fused_computation.1 | convolution fusion | flops 6445334528 | bytes 19922944 | tf_op jit(solution)/shard_map/dot_general | solution.py:33
  406.5 3.4 copy-done.1
  409.9 7.5 %fusion.30 = f32[1024,128]{1,0:T(8,128)} fusion(f32[1024,2048]{1,0:T(8,128)S(1)} %convolution_add_fusion.1, f32[2048,128]{1,0:T(8,128)S(1)} %constant_dynamic-slice_fusion), kind=kOutput, calls=%fused_computation.44 | convolution fusion | flops 3221225472 | bytes 9961472 | tf_op jit(solution)/shard_map/dot_general | solution.py:8
  418.6 3.7 bitcast_subtract_fusion.1
  422.2 2.5 convolution_bitcast_fusion.1
  424.8 14.9 %fusion.34 = f32[2048,128]{1,0:T(8,128)} fusion(f32[1024,2048]{1,0:T(8,128)S(1)} %copy-done.2, f32[1024,128]{1,0:T(8,128)S(1)} %copy-done.4), kind=kOutput, calls=%fused_computation.48 | convolution fusion | flops 3221225472 | bytes 9961472 | tf_op jit(solution)/shard_map/dot_general | solution.py:12
  439.7 48.8 %all-reduce.9.cloned.1.call-done = f32[1024,128]{1,0:T(8,128)} async-done(((f32[1024,128]{1,0:T(8,128)}), f32[1024,128]{1,0:T(8,128)}) %all-reduce.9.cloned.1.call-update) | async-done | bytes 524304 | tf_op jit(solution)/shard_map/psum | solution.py:23
  488.5 2.7 convolution_bitcast_fusion.2
  491.2 2.4 fusion.31
  493.6 144.9 %all-reduce.11.cloned.1.call-done = (f32[2048,128]{1,0:T(8,128)}, f32[128,128]{0,1:T(8,128)}, f32[128,512]{0,1:T(8,128)}) async-done(((f32[2048,128]{1,0:T(8,128)}, f32[128,128]{0,1:T(8,128)}, f32[128,512]{0,1:T(8,128)}), (f32[2048,128]{1,0:T(8,128)}, f32[128,128]{0,1:T(8,128)}, f32[128,512]{0,1:T(8,128)})) %all-reduce.11.cloned.1.call-update) | async-done | bytes 1376272 | tf_op jit(solution)/shard_map/psum | solution.py:25
  638.5 2.2 fusion.20
  640.7 1.0 fusion.32
  642.0 3.2 fusion
  645.2 2.4 fusion.10
  647.6 1.3 fusion.37
  649.0 3.4 bitcast_subtract_fusion
  652.3 2.9 copy.9
  655.2 12.0 %convolution_add_fusion = f32[1024,2048]{1,0:T(8,128)} fusion(f32[1024,2048]{1,0:T(8,128)} %copy-done.1, f32[2048,128]{1,0:T(8,128)} %copy-done.5, f32[2048,128]{1,0:T(8,128)} %fusion, f32[1024,128]{1,0:T(8,128)} %fusion.10, f32[1024,128]{1,0:T(8,128)S(1)} %copy-done.4), kind=kOutput, calls=%fused_computation | convolution fusion | flops 6445334528 | bytes 19922944 | tf_op jit(solution)/shard_map/dot_general | solution.py:33
  (32 shorter events, 5.7 us)
Async XLA Ops:
  7.2 410.8 %copy-start = (f32[128,128]{1,0:T(8,128)S(1)}, f32[128,128]{1,0:T(8,128)}, u32[]{:S(2)}) copy-start(f32[128,128]{1,0:T(8,128)} %param.10) | copy-start | bytes 196612
  7.2 97.6 %copy-start.3 = (f32[1024,128]{1,0:T(8,128)S(1)}, f32[1024,128]{1,0:T(8,128)}, u32[]{:S(2)}) copy-start(f32[1024,128]{1,0:T(8,128)} %param.7) | copy-start | bytes 1572868
  7.2 93.9 %copy-start.4 = (f32[1024,128]{1,0:T(8,128)S(1)}, f32[1024,128]{1,0:T(8,128)}, u32[]{:S(2)}) copy-start(f32[1024,128]{1,0:T(8,128)} %param.9) | copy-start | bytes 1572868
  7.2 79.6 %all-gather.3.cloned.1.call-start = ((), (), s32[]{:S(2)}) async-start(), calls=%async_computation | async-start | bytes 8912896 | tf_op jit(solution)/shard_map/all_gather | solution.py:51
  7.9 159.1 %all-reduce.7.cloned.1.call-start = ((), (), s32[]{:S(2)}) async-start(), calls=%async_computation.1 | async-start | bytes 1048576 | tf_op jit(solution)/shard_map/psum | solution.py:23
  100.1 147.4 %all-gather.5.cloned.1.call-start = ((), (), s32[]{:S(2)}) async-start(), calls=%async_computation.2 | async-start | bytes 8912896 | tf_op jit(solution)/shard_map/all_gather | solution.py:52
  100.8 289.3 %all-reduce.13.cloned.1.call-start = ((), (), s32[]{:S(2)}) async-start(), calls=%async_computation.5 | async-start | bytes 2752512 | tf_op jit(solution)/shard_map/psum | solution.py:25
  121.1 127.6 %copy-start.6 = (f32[128,128]{1,0:T(8,128)S(1)}, f32[128,128]{1,0:T(8,128)}, u32[]{:S(2)}) copy-start(f32[128,128]{1,0:T(8,128)} %param.8) | copy-start | bytes 196612
  169.3 319.2 %all-reduce.9.cloned.1.call-start = ((), (), s32[]{:S(2)}) async-start(), calls=%async_computation.3 | async-start | bytes 1048576 | tf_op jit(solution)/shard_map/psum | solution.py:23
  248.8 157.7 %copy-start.5 = (f32[2048,128]{1,0:T(8,128)}, f32[2048,128]{1,0:T(8,128)S(1)}, u32[]{:S(2)}) copy-start(f32[2048,128]{1,0:T(8,128)S(1)} %constant_dynamic-slice_fusion) | copy-start | bytes 3145732
  406.5 3.4 copy-start.1
  409.9 8.1 %copy-start.7 = (f32[128,512]{1,0:T(8,128)S(1)}, f32[128,512]{1,0:T(8,128)}, u32[]{:S(2)}) copy-start(f32[128,512]{1,0:T(8,128)} %get-tuple-element.9) | copy-start | bytes 786436
  417.4 221.0 %all-reduce.11.cloned.1.call-start = ((), (), s32[]{:S(2)}) async-start(), calls=%async_computation.4 | async-start | bytes 2752512 | tf_op jit(solution)/shard_map/psum | solution.py:25
  418.0 6.8 %copy-start.2 = (f32[1024,2048]{1,0:T(8,128)S(1)}, f32[1024,2048]{1,0:T(8,128)}, u32[]{:S(2)}) copy-start(f32[1024,2048]{1,0:T(8,128)} %copy-done.1) | copy-start | bytes 25165828
Sparse Core Ops, SparseCore 0:
  10.4 76.3 all-gather.2
  100.2 66.7 all-reduce.6
  169.7 77.7 all-gather.4
  250.8 139.3 all-reduce.12
  417.6 70.8 all-reduce.8
  491.6 146.7 all-reduce.10
where the time goes:
time: 678 us; the launch traced here: 674 us
  waiting for transfers between devices  533 us (79%)
  matrix products  114 us (17%)
  between operations  14.5 us (2%)
  local copies, waits for them, and re-layouts  11.8 us (2%)
    psum x2, waiting for transfers between devices, transform(): summed_cols = lax.psum(partial_cols, 'row')  283 us
    psum x2, waiting for transfers between devices, transform(): summed_rows = lax.psum(partial_rows, 'col')  94.7 us
    all_gather x1, waiting for transfers between devices, shards(): lax.all_gather(first_reflector, 'row', axis=0, tiled=True)  78.8 us
    all_gather x1, waiting for transfers between devices, shards(): lax.all_gather(second_reflector, 'row', axis=0, tiled=True)  75 us
    dot_general x18, matrix products, multiply(): jnp.dot(left, right, precision=lax.Precision.HIGHEST, preferred_element_t...  49.3 us
    dot_general x6, matrix products, inner_rows(): lax.dot_general(left, right, (((0,), (0,)), ((), ())), precision=lax.Prec...  42.4 us
    dot_general x2, matrix products, transform(): lax.dot_general(left, right, (((1,), (1,)), ((), ())), precision=lax.Prec...  22.1 us
  transfers between devices with their start and end apart: 6, of which 6 were waited for; matrix products, arithmetic and copies ran while one was open for 8% of the time, Pallas kernels for 0%

commit v1 on v0

v1 whole, which is shorter than its diff:
```python
import jax
import jax.numpy as jnp
from jax import lax
from jax.sharding import PartitionSpec as P

HIGH = lax.Precision.HIGH
BOTH = ("row", "col")
PAIRS = [[2 * i, 2 * i + 1] for i in range(8)]
SAME_CORE = [[2 * i + k for i in range(8)] for k in range(2)]


def dot(left, right, dims=((1,), (0,)), precision=HIGH):
    return lax.dot_general(left, right, (dims, ((), ())), precision=precision, preferred_element_type=jnp.float32)


def small(left, right, dims=((1,), (0,))):
    return dot(left, right, dims, lax.Precision.HIGHEST)


def swap_cores(value):
    return lax.ppermute(value, "row", [(i, i ^ 1) for i in range(16)])


def fetch_map(offset, flip):
    pairs = []
    for x in range(4):
        for y in range(4):
            for zh in range(2):
                for zl in range(2):
                    for k in range(2):
                        xt, yt, zht, zlt = (y - offset - x) % 4, x, (zl + flip) % 2, zh
                        xt = (y - x - offset) % 4
                        pairs.append((((x * 2 + zh) * 2 + k) * 8 + y * 2 + zl, ((xt * 2 + zht) * 2 + k) * 8 + yt * 2 + zlt))
    return sorted(pairs)


def turn_map():
    return [((2 * j + k) * 8 + c, (2 * c + k) * 8 + j) for j in range(8) for k in range(2) for c in range(8)]


def exchange(value, axis, groups):
    return lax.all_to_all(value, axis, 0, 0, tiled=True, axis_index_groups=groups)


def copies(value, times):
    return jnp.broadcast_to(value[None], (times,) + value.shape).reshape((times * value.shape[0],) + value.shape[1:])


def shards(matrix, v1, f1, v2, f2, vectors):
    core = lax.axis_index("row") % 2
    col = lax.axis_index("col")
    half1 = lax.ppermute(v1, BOTH, fetch_map(0, 0))
    half2 = lax.ppermute(v2, BOTH, fetch_map(2, 1))
    own = jnp.concatenate([v1, v2], axis=1)

    part = -dot(matrix, own, ((0,), (0,)))
    cross = small(v1, v2, ((0,), (0,)))
    cross = jnp.concatenate([cross, jnp.zeros_like(cross)], axis=1)

    sums = dot(own, vectors, ((0,), (0,)))
    sums = lax.psum_scatter(sums, "row", scatter_dimension=0, tiled=True)
    sums = lax.all_gather(sums, "row", axis=0, tiled=True)

    rows = part.shape[0] // 2
    part = jnp.concatenate([part.reshape(2, rows, 256), cross.reshape(2, 64, 256)], axis=1)
    part = exchange(part, "row", PAIRS).sum(0)
    p_part, c_part = part[:rows].reshape(8, 128, 256), part[rows:].reshape(8, 8, 256)
    part = jnp.concatenate([p_part, c_part], axis=1)
    part = exchange(part, "row", SAME_CORE).sum(0)
    p_own, c_own = part[:128], part[128:]

    turned = lax.ppermute(p_own, BOTH, turn_map())
    p_rows = exchange(copies(turned[None], 8), "col", None).reshape(1024, 256)
    gram = dot(own, p_rows, ((0,), (0,)))
    gram = lax.dynamic_slice_in_dim(gram, col * 32, 32, 0)

    got = exchange(copies(jnp.concatenate([p_own, c_own, gram], axis=0)[None], 8), "row", SAME_CORE)
    half_gram = got[:, 136:].sum(0)
    mine = jnp.concatenate([got[:, :128].reshape(1024, 256), got[:, 128:136].reshape(64, 256), half_gram], axis=0)
    theirs = swap_cores(mine)
    half_v = jnp.concatenate([half1, half2], axis=1)
    other_v = swap_cores(half_v)

    def ordered(a, b):
        return jnp.concatenate([jnp.where(core == 0, a, b), jnp.where(core == 0, b, a)], axis=0)

    p_cols = ordered(mine[:1024], theirs[:1024])
    c = ordered(mine[1024:1088], theirs[1024:1088])[:, :128]
    v_cols = ordered(half_v, other_v)
    gram = mine[1088:] + theirs[1088:]
    gram = exchange(copies(gram[None], 8), "col", None).reshape(256, 256)

    zero = jnp.zeros_like(c)
    g11, g21, g22 = gram[:128, :128], gram[128:, :128], gram[128:, 128:]
    x1 = small(small(f1.T, g11), f1)
    x1c = small(x1, c)
    d = small(f1.T, g21.T) - 0.5 * small(x1.T, c) + 0.5 * x1c
    f1c = small(f1, c)
    g22 = g22 - small(g21, f1c) + small(c.T, d)
    x2 = small(small(f2.T, g22), f2)
    a_right = -small(f1c, f2)
    b_right = small(d, f2)
    a = jnp.concatenate([jnp.concatenate([f1, a_right], 1), jnp.concatenate([zero, f2], 1)], 0)
    b = jnp.concatenate([jnp.concatenate([-0.5 * x1, b_right], 1), jnp.concatenate([zero, -0.5 * x2], 1)], 0)

    left = jnp.concatenate([dot(own, a, ((1,), (1,))), -dot(p_rows, a) - dot(own, b - b.T)], axis=1)
    right = jnp.concatenate([p_cols, v_cols], axis=1)
    updated = matrix + dot(left, right, ((1,), (1,)))

    t2 = small(f2, sums[128:])
    t1 = small(f1, sums[:128] - small(c, t2))
    back = vectors - dot(own, jnp.concatenate([t1, t2], axis=0))
    return updated, back


def solution(mesh):
    in_specs = (P("row", "col"), P("row", None), P(), P("row", None), P(), P("row", "col"))
    out_specs = (P("row", "col"), P("row", "col"))
    return jax.shard_map(shards, mesh=mesh, in_specs=in_specs, out_specs=out_specs, check_vma=False)
```

time: 678 us -> 258 us (0.38)
  waiting for transfers between devices: 533 us -> 64.2 us
  matrix products: 114 us -> 49.3 us
  blocking collectives: 0 us -> 56.5 us
  starting transfers between devices: 1.09 us -> 41 us
  other arithmetic: 0 us -> 11.8 us
  local copies, waits for them, and re-layouts: 11.8 us -> 19.7 us
    psum x4 -> x0, waiting for transfers between devices: 378 us -> none  [the longest x2 283 us: transform(): summed_cols = lax.psum(partial_cols, 'row')]
    all_gather x2 -> x0, waiting for transfers between devices: 154 us -> none  [the longest x1 78.8 us: shards(): lax.all_gather(first_reflector, 'row', axis=0, tiled=True)]
    dot_general x26 -> x24, matrix products: 114 us -> 49.3 us  [dot(): lax.dot_general(left, right, (dims, ((), ())), precision=precision, prefe...]
    reduce_scatter x0 -> x1, waiting for transfers between devices: none -> 34 us  [shards(): sums = lax.psum_scatter(sums, 'row', scatter_dimension=0, tiled=True)]
    all_to_all x0 -> x2, blocking collectives: none -> 30.9 us  [exchange(): lax.all_to_all(value, axis, 0, 0, tiled=True, axis_index_groups=groups)]
    all_to_all x0 -> x3, starting transfers between devices: none -> 26.1 us  [exchange(): lax.all_to_all(value, axis, 0, 0, tiled=True, axis_index_groups=groups)]
    all_gather x0 -> x1, blocking collectives: none -> 25.7 us  [shards(): sums = lax.all_gather(sums, 'row', axis=0, tiled=True)]
    ppermute x0 -> x5, waiting for transfers between devices: none -> 15.6 us  [the longest x1 15.6 us: shards(): half2 = lax.ppermute(v2, BOTH, fetch_map(2, 1))]
  transfers between devices with their start and end apart: 6 -> 9, of which waited for: 6 -> 3; matrix products, arithmetic and copies ran while one was open for 8% -> 10% of each run, Pallas kernels for 0% -> 0%
where the time goes in v1:
time: 258 us; the launch traced here: 257 us
  waiting for transfers between devices  64.2 us (25%)
  blocking collectives  56.5 us (22%)
  matrix products  49.3 us (19%)
  starting transfers between devices  41 us (16%)
  local copies, waits for them, and re-layouts  19.7 us (8%)
  between operations  14.6 us (6%)
  other arithmetic  11.8 us (5%)
    dot_general x24, matrix products, dot(): lax.dot_general(left, right, (dims, ((), ())), precision=precision, prefe...  49.3 us
    reduce_scatter x1, waiting for transfers between devices, shards(): sums = lax.psum_scatter(sums, 'row', scatter_dimension=0, tiled=True)  34 us
    all_to_all x2, blocking collectives, exchange(): lax.all_to_all(value, axis, 0, 0, tiled=True, axis_index_groups=groups)  30.9 us
    all_to_all x3, starting transfers between devices, exchange(): lax.all_to_all(value, axis, 0, 0, tiled=True, axis_index_groups=groups)  26.1 us
    all_gather x1, blocking collectives, shards(): sums = lax.all_gather(sums, 'row', axis=0, tiled=True)  25.7 us
    ppermute x1, waiting for transfers between devices, shards(): half2 = lax.ppermute(v2, BOTH, fetch_map(2, 1))  15.6 us
    all_to_all x3, waiting for transfers between devices, exchange(): lax.all_to_all(value, axis, 0, 0, tiled=True, axis_index_groups=groups)  14.5 us
    unnamed x51, local copies, waits for them, and re-layouts  8.02 us
  transfers between devices with their start and end apart: 9, of which 3 were waited for; matrix products, arithmetic and copies ran while one was open for 10% of the time, Pallas kernels for 0%

profile of v1, /device:TPU:1, one launch (start us, length us, event | category | flops | bytes accessed | tf_op | source)
XLA Modules:
  0.0 257.1 jit_solution(10257867667497365414)
XLA Ops:
  7.2 1.1 constant_dynamic-update-slice_fusion.1
  8.3 2.2 fusion.41
  10.6 7.7 %fusion.11 = f32[2048,256]{0,1:T(8,128)} fusion(f32[1024,256]{1,0:T(8,128)S(1)} %constant_dynamic-update-slice_fusion, f32[1024,2048]{1,0:T(8,128)} %param.6), kind=kOutput, calls=%fused_computation.10 | convolution fusion | flops 3221749760 | bytes 11534336 | tf_op jit(solution)/shard_map/dot_general | solution.py:13
  18.2 1.9 copy.50
  20.4 6.6 %all_to_all.25 = f32[2,1088,256]{2,1,0:T(8,128)S(1)} all-to-all(f32[2,1088,256]{2,1,0:T(8,128)S(1)} %pad_maximum_fusion), channel_id=1, replica_groups={{0,8},{16,24},{32,40},{48,56},{64,72},{80,88},{96,104},{112,120},{1,9},..., dimensions={0} | all-to-all | bytes 4456448 | tf_op jit(solution)/shard_map/all_to_all | solution.py:42
  26.9 1.2 reduce_sum.27
  29.5 24.3 %all_to_all.26 = f32[8,136,256]{2,1,0:T(8,128)S(1)} all-to-all(f32[8,136,256]{2,1,0:T(8,128)S(1)} %pad_maximum_fusion.2), channel_id=1, replica_groups={{0,16,32,48,64,80,96,112},{8,24,40,56,72,88,104,120},{1,17,33,49,65,81,..., dimensions={0} | all-to-all | bytes 2228224 | tf_op jit(solution)/shard_map/all_to_all | solution.py:42
  55.9 17.3 %all-to-all-start.2 = ((f32[8,128,256]{2,1,0:T(8,128)}), f32[8,128,256]{2,1,0:T(8,128)S(1)}, u32[]{:S(2)}, u32[]{:S(2)}) async-start(f32[8,128,256]{2,1,0:T(8,128)} %reshape.50), calls=%async_computation.2 | async-start | bytes 2097152 | tf_op jit(solution)/shard_map/all_to_all | solution.py:42
  73.2 14.5 %all-to-all-done.2 = f32[8,128,256]{2,1,0:T(8,128)S(1)} async-done(((f32[8,128,256]{2,1,0:T(8,128)}), f32[8,128,256]{2,1,0:T(8,128)S(1)}, u32[]{:S(2)}, u32[]{:S(2)}) %all-to-all-start.2) | async-done | bytes 1048608 | tf_op jit(solution)/shard_map/all_to_all | solution.py:42
  89.0 1.2 reshape.52
  90.2 4.3 %all-to-all-start.3 = ((f32[8,168,256]{2,1,0:T(8,128)}), f32[8,168,256]{2,1,0:T(8,128)}, u32[]{:S(2)}, u32[]{:S(2)}) async-start(f32[8,168,256]{2,1,0:T(8,128)} %reshape.52), calls=%async_computation.3 | async-start | bytes 2752512 | tf_op jit(solution)/shard_map/all_to_all | solution.py:42
  94.5 1.4 collective-permute-start.2
  96.0 7.1 %collective-permute-start.3 = (f32[1024,128]{1,0:T(8,128)S(1)}, f32[1024,128]{1,0:T(8,128)}, u32[]{:S(2)}, u32[]{:S(2)}) collective-permute-start(f32[1024,128]{1,0:T(8,128)S(1)} %copy-done.10), channel_id=1, source_target_pairs={{0,80},{1,64},{2,112},{3,96},{4,16},{5,0},{6,48},{7,32},{8,88},{9,... | collective-permute-start | bytes 1572872 | tf_op jit(solution)/shard_map/ppermute | solution.py:53
  103.1 3.4 %fusion.46 = f32[256,512]{1,0:T(8,128)} fusion(f32[1024,256]{1,0:T(8,128)S(1)} %constant_dynamic-update-slice_fusion, f32[1024,512]{1,0:T(8,128)} %param.11), kind=kOutput, calls=%fused_computation.81 | convolution fusion | flops 805306368 | bytes 3670016 | tf_op jit(solution)/shard_map/dot_general | solution.py:13
  106.5 1.9 constant_dynamic-update-slice_fusion.3
  108.4 15.6 %collective-permute-done.3 = f32[1024,128]{1,0:T(8,128)} collective-permute-done((f32[1024,128]{1,0:T(8,128)S(1)}, f32[1024,128]{1,0:T(8,128)}, u32[]{:S(2)}, u32[]{:S(2)}) %collective-permute-start.3) | collective-permute-done | bytes 524320 | tf_op jit(solution)/shard_map/ppermute | solution.py:53
  124.0 1.9 constant_dynamic-update-slice_fusion.2
  125.9 5.7 %collective-permute-start.4 = (f32[1024,256]{1,0:T(8,128)}, f32[1024,256]{1,0:T(8,128)}, u32[]{:S(2)}, u32[]{:S(2)}) collective-permute-start(f32[1024,256]{1,0:T(8,128)} %constant_dynamic-update-slice_fusion.2), channel_id=1, source_target_pairs={{0,8},{8,0},{16,24},{24,16},{32,40},{40,32},{48,56},{56,48},{64,72... | collective-permute-start | bytes 3145736 | tf_op jit(solution)/shard_map/ppermute | solution.py:21
  132.6 1.4 slice.66
  137.4 34.0 %reduce-scatter.2.cloned.1.call-done = f32[16,512]{1,0:T(8,128)} async-done(((f32[256,512]{1,0:T(8,128)}), f32[16,512]{1,0:T(8,128)}) %reduce-scatter.2.cloned.1.call-update) | async-done | bytes 32784 | tf_op jit(solution)/shard_map/reduce_scatter | solution.py:61
  171.4 25.7 %all_gather.3 = f32[256,512]{1,0:T(8,128)S(1)} all-gather(f32[16,512]{1,0:T(8,128)} %reduce-scatter.2.cloned.1.call-done), channel_id=1, replica_groups=mesh['row'=16,'col'=8] {'row'}, dimensions={0}, use_global_device_ids=true | all-gather | bytes 557056 | tf_op jit(solution)/shard_map/all_gather | solution.py:62
  198.3 3.0 %broadcast_select_fusion.1 = (f32[1024,256]{1,0:T(8,128)}, f32[1024,256]{1,0:T(8,128)}) fusion(f32[1024,256]{1,0:T(8,128)} %constant_dynamic-update-slice_fusion.2, f32[1024,256]{1,0:T(8,128)} %collective-permute-done.4, pred[]{:T(512)S(6)} %eq.4), kind=kLoop, calls=%fused_computation.37 | loop fusion | flops 524288 | bytes 4194305 | tf_op jit(solution)/shard_map/jit(_where)/select_n | solution.py:85
  205.3 4.5 %all-to-all-start.4 = ((f32[8,32,256]{2,1,0:T(8,128)}), f32[8,32,256]{2,1,0:T(8,128)}, u32[]{:S(2)}, u32[]{:S(2)}) async-start(f32[8,32,256]{2,1,0:T(8,128)} %reshape.55), calls=%async_computation.4 | async-start | bytes 524288 | tf_op jit(solution)/shard_map/all_to_all | solution.py:42
  209.8 1.1 convolution_negate_fusion.2
  210.9 1.4 convolution_subtract_fusion.1
  212.7 3.9 %convolution_subtract_fusion = f32[1024,512]{1,0:T(8,128)} fusion(f32[1024,512]{1,0:T(8,128)} %param.11, f32[1024,256]{1,0:T(8,128)S(1)} %constant_dynamic-update-slice_fusion, f32[128,512]{1,0:T(8,128)S(1)} %bitcast.69, f32[128,512]{1,0:T(8,128)S(1)} %convolution_bitcast_fusion), kind=kOutput, calls=%fused_computation.15 | convolution fusion | flops 805961728 | bytes 5767168 | tf_op jit(solution)/shard_map/dot_general | solution.py:13
  216.6 2.7 %slice_select_fusion.1 = (f32[1024,256]{1,0:T(8,128)}, f32[1024,256]{1,0:T(8,128)}) fusion(f32[1120,256]{1,0:T(8,128)} %collective-permute-done.1, pred[]{:T(512)S(6)} %eq.4, f32[8,128,256]{2,1,0:T(8,128)S(1)} %slice.66), kind=kLoop, calls=%fused_computation.32 | loop fusion | flops 524288 | bytes 4194305 | tf_op jit(solution)/shard_map/jit(_where)/select_n | solution.py:85
  220.2 1.1 convolution_subtract_fusion.2
  222.4 1.1 fusion.29
  227.0 1.1 copy.46
  228.1 1.6 fusion.23
  231.6 18.7 %fusion.8 = f32[1024,2048]{1,0:T(8,128)} fusion(f32[1024,2048]{1,0:T(8,128)} %param.6, f32[1024,256]{1,0:T(8,128)S(1)} %copy-done.1, f32[1024,256]{1,0:T(8,128)S(1)} %copy-done, f32[1024,256]{1,0:T(8,128)S(1)} %copy-done.3, f32[1024,256]{1,0:T(8,128)S(1)} %copy-done.2, f32[1024,256]{0,1:T(8,128)S(1)} %fusion.15, f32[1024,256]{0,1:T(8,128)S(1)} %fusion.24), kind=kOutput, calls=%fused_computation.8 | convolution fusion | flops 6448218112 | bytes 23068672 | tf_op jit(solution)/shard_map/dot_general | solution.py:13
  (96 shorter events, 21.9 us)
Async XLA Ops:
  7.2 3.4 %copy-start.9 = (f32[1024,128]{1,0:T(8,128)S(1)}, f32[1024,128]{1,0:T(8,128)}, u32[]{:S(2)}) copy-start(f32[1024,128]{1,0:T(8,128)} %param.9) | copy-start | bytes 1572868
  28.2 1.3 slice-start
  54.0 0.7 collective-permute-start
  55.9 31.8 %all-to-all-start.2 = ((f32[8,128,256]{2,1,0:T(8,128)}), f32[8,128,256]{2,1,0:T(8,128)S(1)}, u32[]{:S(2)}, u32[]{:S(2)}) async-start(f32[8,128,256]{2,1,0:T(8,128)} %reshape.50), calls=%async_computation.2 | async-start | bytes 2097152 | tf_op jit(solution)/shard_map/all_to_all | solution.py:42
  89.0 5.5 %copy-start.8 = (f32[1024,128]{1,0:T(8,128)S(1)}, f32[1024,128]{1,0:T(8,128)}, u32[]{:S(2)}) copy-start(f32[1024,128]{1,0:T(8,128)} %param.7) | copy-start | bytes 1572868
  89.0 7.0 %copy-start.10 = (f32[1024,128]{1,0:T(8,128)S(1)}, f32[1024,128]{1,0:T(8,128)}, u32[]{:S(2)}) copy-start(f32[1024,128]{1,0:T(8,128)} %param.9) | copy-start | bytes 1572868
  90.2 41.4 %all-to-all-start.3 = ((f32[8,168,256]{2,1,0:T(8,128)}), f32[8,168,256]{2,1,0:T(8,128)}, u32[]{:S(2)}, u32[]{:S(2)}) async-start(f32[8,168,256]{2,1,0:T(8,128)} %reshape.52), calls=%async_computation.3 | async-start | bytes 2752512 | tf_op jit(solution)/shard_map/all_to_all | solution.py:42
  94.5 76.9 %reduce-scatter.2.cloned.1.call-start = ((), (), s32[]{:S(2)}) async-start(), calls=%async_computation.6 | async-start | bytes 557056 | tf_op jit(solution)/shard_map/reduce_scatter | solution.py:61
  94.5 12.0 %collective-permute-start.2 = (f32[1024,128]{1,0:T(8,128)S(1)}, f32[1024,128]{1,0:T(8,128)}, u32[]{:S(2)}, u32[]{:S(2)}) collective-permute-start(f32[1024,128]{1,0:T(8,128)S(1)} %copy-done.8), channel_id=1, source_target_pairs={{0,0},{1,16},{2,32},{3,48},{4,64},{5,80},{6,96},{7,112},{8,8},{9,2... | collective-permute-start | bytes 1572872 | tf_op jit(solution)/shard_map/ppermute | solution.py:52
  96.0 28.1 %collective-permute-start.3 = (f32[1024,128]{1,0:T(8,128)S(1)}, f32[1024,128]{1,0:T(8,128)}, u32[]{:S(2)}, u32[]{:S(2)}) collective-permute-start(f32[1024,128]{1,0:T(8,128)S(1)} %copy-done.10), channel_id=1, source_target_pairs={{0,80},{1,64},{2,112},{3,96},{4,16},{5,0},{6,48},{7,32},{8,88},{9,... | collective-permute-start | bytes 1572872 | tf_op jit(solution)/shard_map/ppermute | solution.py:53
  125.9 72.4 %collective-permute-start.4 = (f32[1024,256]{1,0:T(8,128)}, f32[1024,256]{1,0:T(8,128)}, u32[]{:S(2)}, u32[]{:S(2)}) collective-permute-start(f32[1024,256]{1,0:T(8,128)} %constant_dynamic-update-slice_fusion.2), channel_id=1, source_target_pairs={{0,8},{8,0},{16,24},{24,16},{32,40},{40,32},{48,56},{56,48},{64,72... | collective-permute-start | bytes 3145736 | tf_op jit(solution)/shard_map/ppermute | solution.py:21
  132.6 3.3 %copy-start.21 = (f32[32,256]{1,0:T(8,128)}, f32[32,256]{1,0:T(8,128)S(1)}, u32[]{:S(2)}) copy-start(f32[32,256]{1,0:T(8,128)S(1)} %slice_reduce_fusion) | copy-start | bytes 98308
  132.6 3.3 %copy-start.4 = (f32[128,128]{1,0:T(8,128)S(1)}, f32[128,128]{1,0:T(8,128)}, u32[]{:S(2)}) copy-start(f32[128,128]{1,0:T(8,128)} %param.10) | copy-start | bytes 196612
  132.6 4.1 %copy-start.5 = (f32[128,128]{1,0:T(8,128)S(1)}, f32[128,128]{1,0:T(8,128)}, u32[]{:S(2)}) copy-start(f32[128,128]{1,0:T(8,128)} %param.8) | copy-start | bytes 196612
  135.9 65.4 %collective-permute-start.1 = (f32[1120,256]{1,0:T(8,128)}, f32[1120,256]{1,0:T(8,128)}, u32[]{:S(2)}, u32[]{:S(2)}) collective-permute-start(f32[1120,256]{1,0:T(8,128)} %pad_maximum_fusion.1), channel_id=1, source_target_pairs={{0,8},{8,0},{16,24},{24,16},{32,40},{40,32},{48,56},{56,48},{64,72... | collective-permute-start | bytes 3440648 | tf_op jit(solution)/shard_map/ppermute | solution.py:21
  197.1 0.8 copy-start.11
  198.3 5.5 %copy-start.22 = (f32[32,256]{1,0:T(8,128)S(1)}, f32[32,256]{1,0:T(8,128)}, u32[]{:S(2)}) copy-start(f32[32,256]{1,0:T(8,128)} %copy-done.21) | copy-start | bytes 98308
  205.3 14.8 %all-to-all-start.4 = ((f32[8,32,256]{2,1,0:T(8,128)}), f32[8,32,256]{2,1,0:T(8,128)}, u32[]{:S(2)}, u32[]{:S(2)}) async-start(f32[8,32,256]{2,1,0:T(8,128)} %reshape.55), calls=%async_computation.4 | async-start | bytes 524288 | tf_op jit(solution)/shard_map/all_to_all | solution.py:42
  210.9 8.5 %copy-start.12 = (f32[128,128]{0,1:T(8,128)}, f32[128,128]{0,1:T(8,128)S(1)}, u32[]{:S(2)}) copy-start(f32[128,128]{0,1:T(8,128)S(1)} %convolution_negate_fusion.2) | copy-start | bytes 196612
  216.6 2.8 %copy-start.16 = (f32[128,128]{0,1:T(8,128)S(1)}, f32[128,128]{0,1:T(8,128)}, u32[]{:S(2)}) copy-start(f32[128,128]{0,1:T(8,128)} %copy.42) | copy-start | bytes 196612
  216.6 2.8 %copy-start.18 = (f32[128,128]{0,1:T(8,128)S(1)}, f32[128,128]{0,1:T(8,128)}, u32[]{:S(2)}) copy-start(f32[128,128]{0,1:T(8,128)} %copy.41) | copy-start | bytes 196612
  219.4 0.8 copy-start.14
  219.4 4.5 %copy-start.7 = (f32[128,128]{1,0:T(8,128)S(1)}, f32[128,128]{1,0:T(8,128)}, u32[]{:S(2)}) copy-start(f32[128,128]{1,0:T(8,128)} %copy-done.6) | copy-start | bytes 196612
  223.8 1.8 copy-start.20
  224.7 4.9 %copy-start.13 = (f32[128,128]{0,1:T(8,128)S(1)}, f32[128,128]{0,1:T(8,128)}, u32[]{:S(2)}) copy-start(f32[128,128]{0,1:T(8,128)} %copy-done.12) | copy-start | bytes 196612
  225.6 0.6 copy-start.15
  228.1 1.6 copy-start.17
  228.1 1.6 copy-start.19
  228.1 2.3 copy-start.3
  229.7 1.2 copy-start
  229.7 1.5 copy-start.1
  229.7 1.8 copy-start.2
  (1 other events, 0.6 us)
Sparse Core Ops, SparseCore 0:
  106.7 64.7 reduce-scatter.1

commit v2 on v1

v2 whole, which is shorter than its diff:
```python
import jax
import jax.numpy as jnp
from jax import lax
from jax.experimental import pallas as pl
from jax.experimental.pallas import tpu as pltpu
from jax.sharding import PartitionSpec as P

HIGH = lax.Precision.HIGH
BOTH = ("row", "col")
SAME_CORE = [[2 * i + k for i in range(8)] for k in range(2)]
F32 = jnp.float32
BF16 = jnp.bfloat16


def dot(left, right, dims=((1,), (0,)), precision=HIGH):
    return lax.dot_general(left, right, (dims, ((), ())), precision=precision, preferred_element_type=F32)


def small(left, right, dims=((1,), (0,))):
    return dot(left, right, dims, lax.Precision.HIGHEST)


def split(value):
    high = value.astype(BF16)
    return high, (value - high.astype(F32)).astype(BF16)


def mxu(left, right):
    return jnp.dot(left, right, preferred_element_type=F32)


def swap_cores(value):
    return lax.ppermute(value, "row", [(i, i ^ 1) for i in range(16)])


def fetch_map(offset, flip):
    pairs = []
    for x in range(4):
        for y in range(4):
            for zh in range(2):
                for zl in range(2):
                    for k in range(2):
                        xt, yt, zht, zlt = (y - x - offset) % 4, x, (zl + flip) % 2, zh
                        pairs.append((((x * 2 + zh) * 2 + k) * 8 + y * 2 + zl, ((xt * 2 + zht) * 2 + k) * 8 + yt * 2 + zlt))
    return sorted(pairs)


def turn_map():
    return [((2 * j + k) * 8 + c, (2 * c + k) * 8 + j) for j in range(8) for k in range(2) for c in range(8)]


def exchange(value, axis, groups):
    return lax.all_to_all(value, axis, 0, 0, axis_index_groups=groups, tiled=True)


def copies(value, times):
    return jnp.broadcast_to(value[None], (times,) + value.shape)


def half_kernel(which_ref, turned_ref, matrix_ref, out_ref, both_ref):
    @pl.when(pl.program_id(0) == 0)
    def _():
        high, low = split(-turned_ref[...])
        both_ref[:256] = high
        both_ref[256:] = low

    high, low = split(matrix_ref[...])
    first = mxu(both_ref[...], high)
    total = first[:256] + first[256:] + mxu(both_ref[:256], low)
    out_ref[0] = total[:, :128]
    out_ref[1] = total[:, 128:]


def half_product(which, turned, matrix):
    depth = matrix.shape[0]
    return pl.pallas_call(
        half_kernel,
        grid_spec=pltpu.PrefetchScalarGridSpec(
            num_scalar_prefetch=1,
            grid=(4,),
            in_specs=[
                pl.BlockSpec((256, depth), lambda i, which: (0, 0)),
                pl.BlockSpec((depth, 256), lambda i, which: (0, which[0] * 4 + i)),
            ],
            out_specs=pl.BlockSpec((2, 256, 128), lambda i, which: (i, 0, 0)),
            scratch_shapes=[pltpu.VMEM((512, depth), BF16)],
        ),
        out_shape=jax.ShapeDtypeStruct((8, 256, 128), F32),
        compiler_params=pltpu.CompilerParams(vmem_limit_bytes=32 * 2**20),
        cost_estimate=pl.CostEstimate(flops=3 * 2 * 256 * depth * 1024, bytes_accessed=4 * depth * 1024 + 2**20, transcendentals=0),
    )(which, turned, matrix)


def add_kernel(left_ref, right_ref, base_ref, out_ref, wide_ref):
    @pl.when(pl.program_id(0) == 0)
    def _():
        high, low = split(left_ref[...])
        wide_ref[:, :256] = high
        wide_ref[:, 256:512] = low

    high, low = split(jnp.concatenate([right_ref[0], right_ref[1]], axis=1))
    total = mxu(wide_ref[:, :256], high) + mxu(wide_ref[:, 256:], high) + mxu(wide_ref[:, :256], low)
    out_ref[...] = base_ref[...] + total


def add_product(left, right, base):
    rows, cols = base.shape
    return pl.pallas_call(
        add_kernel,
        grid=(cols // 256,),
        in_specs=[
            pl.BlockSpec((rows, 256), lambda i: (0, 0)),
            pl.BlockSpec((2, 256, 128), lambda i: (i, 0, 0)),
            pl.BlockSpec((rows, 256), lambda i: (0, i)),
        ],
        out_specs=pl.BlockSpec((rows, 256), lambda i: (0, i)),
        scratch_shapes=[pltpu.VMEM((rows, 512), BF16)],
        out_shape=jax.ShapeDtypeStruct((rows, cols), F32),
        compiler_params=pltpu.CompilerParams(vmem_limit_bytes=32 * 2**20),
        cost_estimate=pl.CostEstimate(flops=3 * 2 * rows * cols * 256, bytes_accessed=8 * rows * cols, transcendentals=0),
    )(left, right, base)


def shards(matrix, v1, f1, v2, f2, vectors):
    core = lax.axis_index("row") % 2
    chip = lax.axis_index("row") // 2
    col = lax.axis_index("col")

    def of_core(value):
        value = value.reshape((2, value.shape[0] // 2) + value.shape[1:])
        return value[core], value[1 - core]

    def ordered(mine, theirs):
        return jnp.concatenate([jnp.where(core == 0, mine, theirs), jnp.where(core == 0, theirs, mine)], axis=0)

    half1 = lax.ppermute(v1, BOTH, fetch_map(0, 0))
    half2 = lax.ppermute(v2, BOTH, fetch_map(2, 1))
    own = jnp.concatenate([v1, v2], axis=1)
    turned = own.T

    away = half_product((1 - core)[None], turned, matrix)
    came = swap_cores(away)
    kept = half_product(core[None], turned, matrix)

    sums = dot(turned, vectors).reshape(1024, 128)
    sums_kept, sums_away = of_core(sums)
    cross = dot(v1, v2, ((0,), (0,)))
    side = swap_cores(jnp.concatenate([sums_away, cross], axis=0))
    sums_kept = (sums_kept + side[:512]).reshape(8, 64, 128)
    cross = (cross + side[512:]).reshape(8, 16, 128)

    packed = jnp.concatenate([kept + came, sums_kept, cross], axis=1)
    packed = exchange(packed, "row", SAME_CORE).sum(0)

    over = lax.ppermute(packed[:256].T, BOTH, turn_map())
    got = exchange(copies(packed, 8), "row", SAME_CORE)
    half_p = got[:, :256]
    half_v = jnp.concatenate([half1, half2], axis=1)
    gram = dot(
        lax.dynamic_slice_in_dim(half_p, chip * 32, 32, 1).transpose(1, 0, 2).reshape(32, 1024),
        half_v,
    )
    p_rows = exchange(copies(jnp.concatenate([over, gram], axis=0), 8), "col", None)
    gram = p_rows[:, 128:].sum(0)
    p_rows = p_rows[:, :128].reshape(1024, 256)
    gram = gram + swap_cores(gram)
    gram = exchange(copies(gram, 8), "row", SAME_CORE).reshape(256, 256)

    p_cols = ordered(half_p, swap_cores(half_p))
    v_cols = ordered(half_v, swap_cores(half_v))
    half_s = got[:, 256:320].reshape(512, 128)
    sums = ordered(half_s, swap_cores(half_s)).reshape(256, 512)
    cross = got[:, 320:].reshape(128, 128)
    a_right = -small(small(f1, cross), f2)
    factor = jnp.concatenate(
        [jnp.concatenate([f1, a_right], axis=1), jnp.concatenate([jnp.zeros_like(f2), f2], axis=1)], axis=0
    )
    back = vectors - dot(own, dot(factor, sums))
    y_rows = dot(own, factor, ((1,), (1,)))
    y_cols = dot(factor, v_cols, ((1,), (1,))).reshape(256, 16, 128).transpose(1, 0, 2)

    inner = add_product(y_rows, p_cols, matrix)
    updated = add_product(-p_rows - dot(y_rows, gram), y_cols, inner)
    return updated, back


def solution(mesh):
    in_specs = (P("row", "col"), P("row", None), P(), P("row", None), P(), P("row", "col"))
    out_specs = (P("row", "col"), P("row", "col"))
    return jax.shard_map(shards, mesh=mesh, in_specs=in_specs, out_specs=out_specs, check_vma=False)
```

time: 258 us -> 185 us (0.72)
  blocking collectives: 56.5 us -> 0 us
  matrix products: 49.3 us -> 18.9 us
  Pallas kernels: 0 us -> 19.2 us
  waiting for transfers between devices: 64.2 us -> 48.8 us
  local copies, waits for them, and re-layouts: 19.7 us -> 33.4 us
  between operations: 14.6 us -> 1.1 us
  starting transfers between devices: 41 us -> 47.7 us
    reduce_scatter x1 -> x0, waiting for transfers between devices: 34 us -> none  [shards(): sums = lax.psum_scatter(sums, 'row', scatter_dimension=0, tiled=True)]
    all_to_all x2 -> x0, blocking collectives: 30.9 us -> none  [exchange(): lax.all_to_all(value, axis, 0, 0, tiled=True, axis_index_groups=groups)]
    dot_general x24 -> x10, matrix products: 49.3 us -> 18.9 us  [dot(): lax.dot_general(left, right, (dims, ((), ())), precision=precision, prefe...]
    all_gather x1 -> x0, blocking collectives: 25.7 us -> none  [shards(): sums = lax.all_gather(sums, 'row', axis=0, tiled=True)]
    pallas_call x0 -> x4, Pallas kernels: none -> 19.2 us  [the longest x2 13.4 us: add_product(): pl.pallas_call(add_kernel, grid=(cols // 256,), in_specs=[pl.BlockSpec((r...]
    unnamed x51 -> x55, local copies, waits for them, and re-layouts: 8.02 us -> 22.8 us
    all_to_all x3 -> x4, waiting for transfers between devices: 14.5 us -> 25.3 us  [exchange(): lax.all_to_all(value, axis, 0, 0, axis_index_groups=groups, tiled=True)]
    ppermute x1, waiting for transfers between devices: 15.6 us -> 23.5 us  [shards(): half2 = lax.ppermute(v2, BOTH, fetch_map(2, 1))]
  transfers between devices with their start and end apart: 9 -> 13, of which waited for: 3 -> 4; matrix products, arithmetic and copies ran while one was open for 10% -> 21% of each run, Pallas kernels for 0% -> 5%
where the time goes in v2:
time: 185 us; the launch traced here: 183 us
  waiting for transfers between devices  48.8 us (26%)
  starting transfers between devices  47.7 us (26%)
  local copies, waits for them, and re-layouts  33.4 us (18%)
  Pallas kernels  19.2 us (10%)
  matrix products  18.9 us (10%)
  other arithmetic  14.1 us (8%)
    all_to_all x4, starting transfers between devices, exchange(): lax.all_to_all(value, axis, 0, 0, axis_index_groups=groups, tiled=True)  27.9 us
    all_to_all x4, waiting for transfers between devices, exchange(): lax.all_to_all(value, axis, 0, 0, axis_index_groups=groups, tiled=True)  25.3 us
    ppermute x1, waiting for transfers between devices, shards(): half2 = lax.ppermute(v2, BOTH, fetch_map(2, 1))  23.5 us
    unnamed x55, local copies, waits for them, and re-layouts  22.8 us
    dot_general x10, matrix products, dot(): lax.dot_general(left, right, (dims, ((), ())), precision=precision, prefe...  18.9 us
    pallas_call x2, Pallas kernels, add_product(): pl.pallas_call(add_kernel, grid=(cols // 256,), in_specs=[pl.BlockSpec((r...  13.4 us
    ppermute x1, starting transfers between devices, shards(): half2 = lax.ppermute(v2, BOTH, fetch_map(2, 1))  9.12 us
    ppermute x6, starting transfers between devices, swap_cores(): return lax.ppermute(value, 'row', [(i, i ^ 1) for i in range(16)])  7.83 us
  transfers between devices with their start and end apart: 13, of which 4 were waited for; matrix products, arithmetic and copies ran while one was open for 21% of the time, Pallas kernels for 5%

profile of v2, /device:TPU:1, one launch (start us, length us, event | category | flops | bytes accessed | tf_op | source)
XLA Modules:
  0.0 183.3 jit_solution(15014035133360488794)
XLA Ops:
  3.5 3.5 %copy-done = f32[1024,2048]{1,0:T(8,128)S(1)} copy-done((f32[1024,2048]{1,0:T(8,128)S(1)}, f32[1024,2048]{1,0:T(8,128)}, u32[]{:S(2)}) %copy-start) | copy-done | bytes 8388632
  6.9 2.9 %shard_map.78 = f32[8,256,128]{2,1,0:T(8,128)S(1)} custom-call(s32[1]{0:T(128)} %bitcast.2.which_ref, f32[256,1024]{1,0:T(8,128)S(1)} %fusion.6.turned_ref, f32[1024,2048]{1,0:T(8,128)S(1)} %copy-done), custom_call_target="tpu_custom_call" | custom-call | flops 1610612736 | bytes 5242880 | tf_op jit(solution)/shard_map/pallas_call | solution.py:76
  11.4 1.9 %fusion.5 = f32[256,512]{1,0:T(8,128)} fusion(f32[1024,512]{1,0:T(8,128)S(1)} %copy-done.10, f32[1024,128]{0,1:T(8,128)S(1)} %copy.15, f32[1024,128]{0,1:T(8,128)S(1)} %copy.14), kind=kOutput, calls=%fused_computation.17 | convolution fusion | flops 805568512 | bytes 3670016 | tf_op jit(solution)/shard_map/dot_general | solution.py:16
  15.1 3.4 %copy-done.1 = f32[1024,2048]{1,0:T(8,128)S(1)} copy-done((f32[1024,2048]{1,0:T(8,128)S(1)}, f32[1024,2048]{1,0:T(8,128)}, u32[]{:S(2)}) %copy-start.1) | copy-done | bytes 8388632
  18.5 2.9 %shard_map.77 = f32[8,256,128]{2,1,0:T(8,128)S(1)} custom-call(s32[1]{0:T(128)} %bitcast.which_ref, f32[256,1024]{1,0:T(8,128)S(1)} %fusion.6.turned_ref, f32[1024,2048]{1,0:T(8,128)S(1)} %copy-done.1), custom_call_target="tpu_custom_call" | custom-call | flops 1610612736 | bytes 5242880 | tf_op jit(solution)/shard_map/pallas_call | solution.py:76
  24.0 7.4 %all-to-all-start = ((f32[8,336,128]{2,1,0:T(8,128)}), f32[8,336,128]{2,1,0:T(8,128)S(1)}, u32[]{:S(2)}, u32[]{:S(2)}) async-start(f32[8,336,128]{2,1,0:T(8,128)} %pad_maximum_fusion.1), calls=%async_computation | async-start | bytes 2752512 | tf_op jit(solution)/shard_map/all_to_all | solution.py:53
  32.2 9.1 %collective-permute-start.4 = (f32[1024,128]{1,0:T(8,128)S(1)}, f32[1024,128]{1,0:T(8,128)S(1)}, u32[]{:S(2)}, u32[]{:S(2)}) collective-permute-start(f32[1024,128]{1,0:T(8,128)S(1)} %copy-done.15), channel_id=1, source_target_pairs={{0,80},{1,64},{2,112},{3,96},{4,16},{5,0},{6,48},{7,32},{8,88},{9,... | collective-permute-start | bytes 1572872 | tf_op jit(solution)/shard_map/ppermute | solution.py:137
  41.3 23.5 %collective-permute-done.4 = f32[1024,128]{1,0:T(8,128)S(1)} collective-permute-done((f32[1024,128]{1,0:T(8,128)S(1)}, f32[1024,128]{1,0:T(8,128)S(1)}, u32[]{:S(2)}, u32[]{:S(2)}) %collective-permute-start.4) | collective-permute-done | bytes 524320 | tf_op jit(solution)/shard_map/ppermute | solution.py:137
  64.9 2.7 %collective-permute-start.6 = (f32[1024,256]{1,0:T(8,128)S(1)}, f32[1024,256]{1,0:T(8,128)}, u32[]{:S(2)}, u32[]{:S(2)}) collective-permute-start(f32[1024,256]{1,0:T(8,128)S(1)} %constant_dynamic-update-slice_fusion), channel_id=1, source_target_pairs={{0,8},{8,0},{16,24},{24,16},{32,40},{40,32},{48,56},{56,48},{64,72... | collective-permute-start | bytes 3145736 | tf_op jit(solution)/shard_map/ppermute | solution.py:33
  68.8 10.6 %all-to-all-start.1 = ((f32[8,336,128]{2,1,0:T(8,128)}), f32[8,336,128]{2,1,0:T(8,128)S(1)}, u32[]{:S(2)}, u32[]{:S(2)}) async-start(f32[8,336,128]{2,1,0:T(8,128)} %broadcast_in_dim.12), calls=%async_computation.1 | async-start | bytes 2752512 | tf_op jit(solution)/shard_map/all_to_all | solution.py:53
  80.8 2.4 %broadcast_select_fusion.3 = (f32[1024,256]{1,0:T(8,128)S(1)}, f32[1024,256]{1,0:T(8,128)}) fusion(f32[1024,256]{1,0:T(8,128)S(1)} %constant_dynamic-update-slice_fusion, f32[1024,256]{1,0:T(8,128)} %collective-permute-done.6, pred[]{:T(512)S(6)} %eq.4), kind=kLoop, calls=%fused_computation.15 | loop fusion | flops 524288 | bytes 4194305 | tf_op jit(solution)/shard_map/jit(_where)/select_n | solution.py:134
  83.9 2.1 %collective-permute-start.2 = (f32[128,256]{0,1:T(8,128)}, f32[128,256]{0,1:T(8,128)}, u32[]{:S(2)}, u32[]{:S(2)}) collective-permute-start(f32[128,256]{0,1:T(8,128)} %slice_bitcast_fusion), channel_id=1, source_target_pairs={{0,0},{1,16},{2,32},{3,48},{4,64},{5,80},{6,96},{7,112},{8,8},{9,2... | collective-permute-start | bytes 393224 | tf_op jit(solution)/shard_map/ppermute | solution.py:155
  86.0 14.7 %all-to-all-done.1 = f32[8,336,128]{2,1,0:T(8,128)S(1)} async-done(((f32[8,336,128]{2,1,0:T(8,128)}), f32[8,336,128]{2,1,0:T(8,128)S(1)}, u32[]{:S(2)}, u32[]{:S(2)}) %all-to-all-start.1) | async-done | bytes 1376288 | tf_op jit(solution)/shard_map/all_to_all | solution.py:53
  103.1 1.9 %collective-permute-start.8 = (f32[512,128]{1,0:T(8,128)}, f32[512,128]{1,0:T(8,128)}, u32[]{:S(2)}, u32[]{:S(2)}) collective-permute-start(f32[512,128]{1,0:T(8,128)} %bitcast.14), channel_id=1, source_target_pairs={{0,8},{8,0},{16,24},{24,16},{32,40},{40,32},{48,56},{56,48},{64,72... | collective-permute-start | bytes 786440 | tf_op jit(solution)/shard_map/ppermute | solution.py:33
  106.1 2.6 %fusion.7 = f32[32,256]{0,1:T(8,128)} fusion(f32[1024,256]{1,0:T(8,128)S(1)} %constant_dynamic-update-slice_fusion, f32[8,256,128]{2,1,0:T(8,128)} %slice.35, s32[]{:T(128)S(6)} %select_n.60), kind=kOutput, calls=%fused_computation.26 | convolution fusion | flops 50331648 | bytes 1212420 | tf_op jit(solution)/shard_map/dot_general | solution.py:16
  108.6 2.4 %fusion = f32[256,2048]{0,1:T(8,128)} fusion(f32[1024,256]{1,0:T(8,128)S(1)} %copy-done.11, f32[1024,256]{1,0:T(8,128)S(1)} %get-tuple-element.4, f32[128,128]{0,1:T(8,128)S(1)} %copy-done.20, f32[128,128]{0,1:T(8,128)S(1)} %convolution_negate_fusion, f32[128,128]{0,1:T(8,128)S(1)} %copy-done.18), kind=kOutput, calls=%fused_computation | convolution fusion | flops 806092800 | bytes 4390912 | tf_op jit(solution)/shard_map/dot_general | solution.py:16
  111.0 1.9 %copy.22 = f32[256,16,128]{2,0,1:T(8,128)S(1)} copy(f32[256,16,128]{0,2,1:T(8,128)} %bitcast.41) | data formatting | bytes 4194304 | tf_op jit(solution)/shard_map/reshape | solution.py:180
  115.2 5.2 %all-to-all-start.2 = ((f32[8,160,256]{2,1,0:T(8,128)}), f32[8,160,256]{2,1,0:T(8,128)}, u32[]{:S(2)}, u32[]{:S(2)}) async-start(f32[8,160,256]{2,1,0:T(8,128)} %broadcast_in_dim.13), calls=%async_computation.2 | async-start | bytes 2621440 | tf_op jit(solution)/shard_map/all_to_all | solution.py:53
  120.4 2.2 %fusion.4.left_ref = f32[1024,256]{1,0:T(8,128)S(1)} fusion(f32[1024,128]{0,1:T(8,128)} %copy-done.7, f32[1024,128]{0,1:T(8,128)} %copy-done.6, f32[128,128]{0,1:T(8,128)S(1)} %copy-done.21, f32[128,128]{0,1:T(8,128)S(1)} %convolution_negate_fusion, f32[128,128]{0,1:T(8,128)S(1)} %copy-done.19), kind=kOutput, calls=%fused_computation.16 | convolution fusion | flops 403177472 | bytes 2293760 | tf_op jit(solution)/shard_map/dot_general | solution.py:16
  124.6 1.9 %reshape.40 = f32[256,512]{1,0:T(8,128)} reshape(f32[1024,128]{1,0:T(8,128)} %pad_maximum_fusion.3) | data formatting | bytes 1048576 | tf_op jit(solution)/shard_map/reshape | solution.py:172
  128.0 4.4 %convolution_subtract_fusion = f32[1024,512]{1,0:T(8,128)} fusion(f32[1024,512]{1,0:T(8,128)} %param.11, f32[256,512]{1,0:T(8,128)S(1)} %fusion.10, f32[1024,128]{0,1:T(8,128)} %copy-done.7, f32[1024,128]{0,1:T(8,128)} %copy-done.6), kind=kOutput, calls=%fused_computation.5 | convolution fusion | flops 806092800 | bytes 5767168 | tf_op jit(solution)/shard_map/dot_general | solution.py:16
  135.3 4.7 %all-to-all-done.2 = f32[8,160,256]{2,1,0:T(8,128)} async-done(((f32[8,160,256]{2,1,0:T(8,128)}), f32[8,160,256]{2,1,0:T(8,128)}, u32[]{:S(2)}, u32[]{:S(2)}) %all-to-all-start.2) | async-done | bytes 1310752 | tf_op jit(solution)/shard_map/all_to_all | solution.py:53
  141.0 1.6 collective-permute-start.5
  142.6 3.4 %copy-done.2 = f32[1024,2048]{1,0:T(8,128)S(1)} copy-done((f32[1024,2048]{1,0:T(8,128)S(1)}, f32[1024,2048]{1,0:T(8,128)}, u32[]{:S(2)}) %copy-start.2) | copy-done | bytes 8388632
  147.6 6.1 %shard_map.79.base_ref = f32[1024,2048]{1,0:T(8,128)S(1)} custom-call(f32[1024,256]{1,0:T(8,128)S(1)} %fusion.4.left_ref, f32[16,256,128]{2,1,0:T(8,128)S(1)} %copy-done.5, f32[1024,2048]{1,0:T(8,128)S(1)} %copy-done.2), custom_call_target="tpu_custom_call" | custom-call | flops 3221225472 | bytes 16777216 | tf_op jit(solution)/shard_map/pallas_call | solution.py:108
  153.7 3.4 %copy-done.3 = f32[1024,2048]{1,0:T(8,128)} copy-done((f32[1024,2048]{1,0:T(8,128)}, f32[1024,2048]{1,0:T(8,128)S(1)}, u32[]{:S(2)}) %copy-start.3) | copy-done | bytes 8388632
  157.8 4.7 %all-to-all-start.3 = ((f32[8,32,256]{2,1,0:T(8,128)}), f32[8,32,256]{2,1,0:T(8,128)S(1)}, u32[]{:S(2)}, u32[]{:S(2)}) async-start(f32[8,32,256]{2,1,0:T(8,128)} %broadcast_in_dim.14), calls=%async_computation.3 | async-start | bytes 524288 | tf_op jit(solution)/shard_map/all_to_all | solution.py:53
  162.5 2.3 %slice_negate_fusion = f32[8,128,256]{2,1,0:T(8,128)} fusion(f32[8,160,256]{2,1,0:T(8,128)} %all-to-all-done.2), kind=kLoop, calls=%fused_computation.9 | loop fusion | flops 262144 | bytes 2097152 | tf_op jit(solution)/shard_map/neg | solution.py:183
  164.8 5.9 %all-to-all-done.3 = f32[8,32,256]{2,1,0:T(8,128)S(1)} async-done(((f32[8,32,256]{2,1,0:T(8,128)}), f32[8,32,256]{2,1,0:T(8,128)S(1)}, u32[]{:S(2)}, u32[]{:S(2)}) %all-to-all-start.3) | async-done | bytes 262176 | tf_op jit(solution)/shard_map/all_to_all | solution.py:53
  170.7 1.8 convolution_subtract_fusion.1.left_ref
  172.6 3.4 %copy-done.4 = f32[1024,2048]{1,0:T(8,128)S(1)} copy-done((f32[1024,2048]{1,0:T(8,128)S(1)}, f32[1024,2048]{1,0:T(8,128)}, u32[]{:S(2)}) %copy-start.4) | copy-done | bytes 8388632
  175.9 7.4 %shard_map.80 = f32[1024,2048]{1,0:T(8,128)} custom-call(f32[1024,256]{1,0:T(8,128)S(1)} %convolution_subtract_fusion.1.left_ref, f32[16,256,128]{2,1,0:T(8,128)S(1)} %bitcast.40, f32[1024,2048]{1,0:T(8,128)S(1)} %copy-done.4), custom_call_target="tpu_custom_call" | custom-call | flops 3221225472 | bytes 16777216 | tf_op jit(solution)/shard_map/pallas_call | solution.py:108
  (92 shorter events, 28.1 us)
Async XLA Ops:
  1.9 9.5 %copy-start.6 = (f32[1024,128]{0,1:T(8,128)}, f32[1024,128]{0,1:T(8,128)S(1)}, u32[]{:S(2)}) copy-start(f32[1024,128]{0,1:T(8,128)S(1)} %copy.14) | copy-start | bytes 1572868
  3.3 8.0 %copy-start.7 = (f32[1024,128]{0,1:T(8,128)}, f32[1024,128]{0,1:T(8,128)S(1)}, u32[]{:S(2)}) copy-start(f32[1024,128]{0,1:T(8,128)S(1)} %copy.15) | copy-start | bytes 1572868
  3.5 3.5 %copy-start = (f32[1024,2048]{1,0:T(8,128)S(1)}, f32[1024,2048]{1,0:T(8,128)}, u32[]{:S(2)}) copy-start(f32[1024,2048]{1,0:T(8,128)} %base_ref.1) | copy-start | bytes 25165828
  6.9 4.5 %copy-start.10 = (f32[1024,512]{1,0:T(8,128)S(1)}, f32[1024,512]{1,0:T(8,128)}, u32[]{:S(2)}) copy-start(f32[1024,512]{1,0:T(8,128)} %param.11) | copy-start | bytes 6291460
  9.8 3.4 %copy-start.12 = (f32[1024,128]{1,0:T(8,128)S(1)}, f32[1024,128]{1,0:T(8,128)}, u32[]{:S(2)}) copy-start(f32[1024,128]{1,0:T(8,128)} %param.7) | copy-start | bytes 1572868
  9.8 3.4 %copy-start.14 = (f32[1024,128]{1,0:T(8,128)S(1)}, f32[1024,128]{1,0:T(8,128)}, u32[]{:S(2)}) copy-start(f32[1024,128]{1,0:T(8,128)} %param.9) | copy-start | bytes 1572868
  9.9 11.6 %collective-permute-start = (f32[8,256,128]{2,1,0:T(8,128)S(1)}, f32[8,256,128]{2,1,0:T(8,128)}, u32[]{:S(2)}, u32[]{:S(2)}) collective-permute-start(f32[8,256,128]{2,1,0:T(8,128)S(1)} %shard_map.78), channel_id=1, source_target_pairs={{0,8},{8,0},{16,24},{24,16},{32,40},{40,32},{48,56},{56,48},{64,72... | collective-permute-start | bytes 3145736 | tf_op jit(solution)/shard_map/ppermute | solution.py:33
  15.0 6.4 %collective-permute-start.1 = (f32[640,128]{1,0:T(8,128)S(1)}, f32[640,128]{1,0:T(8,128)S(1)}, u32[]{:S(2)}, u32[]{:S(2)}) collective-permute-start(f32[640,128]{1,0:T(8,128)S(1)} %pad_maximum_fusion.7), channel_id=1, source_target_pairs={{0,8},{8,0},{16,24},{24,16},{32,40},{40,32},{48,56},{56,48},{64,72... | collective-permute-start | bytes 983048 | tf_op jit(solution)/shard_map/ppermute | solution.py:33
  22.8 8.6 %copy-start.13 = (f32[1024,128]{1,0:T(8,128)S(1)}, f32[1024,128]{1,0:T(8,128)}, u32[]{:S(2)}) copy-start(f32[1024,128]{1,0:T(8,128)} %param.7) | copy-start | bytes 1572868
  22.9 9.3 %copy-start.15 = (f32[1024,128]{1,0:T(8,128)S(1)}, f32[1024,128]{1,0:T(8,128)}, u32[]{:S(2)}) copy-start(f32[1024,128]{1,0:T(8,128)} %param.9) | copy-start | bytes 1572868
  24.0 43.5 %all-to-all-start = ((f32[8,336,128]{2,1,0:T(8,128)}), f32[8,336,128]{2,1,0:T(8,128)S(1)}, u32[]{:S(2)}, u32[]{:S(2)}) async-start(f32[8,336,128]{2,1,0:T(8,128)} %pad_maximum_fusion.1), calls=%async_computation | async-start | bytes 2752512 | tf_op jit(solution)/shard_map/all_to_all | solution.py:53
  31.5 9.8 %collective-permute-start.3 = (f32[1024,128]{1,0:T(8,128)S(1)}, f32[1024,128]{1,0:T(8,128)S(1)}, u32[]{:S(2)}, u32[]{:S(2)}) collective-permute-start(f32[1024,128]{1,0:T(8,128)S(1)} %copy-done.13), channel_id=1, source_target_pairs={{0,0},{1,16},{2,32},{3,48},{4,64},{5,80},{6,96},{7,112},{8,8},{9,2... | collective-permute-start | bytes 1572872 | tf_op jit(solution)/shard_map/ppermute | solution.py:136
  32.2 32.7 %collective-permute-start.4 = (f32[1024,128]{1,0:T(8,128)S(1)}, f32[1024,128]{1,0:T(8,128)S(1)}, u32[]{:S(2)}, u32[]{:S(2)}) collective-permute-start(f32[1024,128]{1,0:T(8,128)S(1)} %copy-done.15), channel_id=1, source_target_pairs={{0,80},{1,64},{2,112},{3,96},{4,16},{5,0},{6,48},{7,32},{8,88},{9,... | collective-permute-start | bytes 1572872 | tf_op jit(solution)/shard_map/ppermute | solution.py:137
  64.9 16.0 %collective-permute-start.6 = (f32[1024,256]{1,0:T(8,128)S(1)}, f32[1024,256]{1,0:T(8,128)}, u32[]{:S(2)}, u32[]{:S(2)}) collective-permute-start(f32[1024,256]{1,0:T(8,128)S(1)} %constant_dynamic-update-slice_fusion), channel_id=1, source_target_pairs={{0,8},{8,0},{16,24},{24,16},{32,40},{40,32},{48,56},{56,48},{64,72... | collective-permute-start | bytes 3145736 | tf_op jit(solution)/shard_map/ppermute | solution.py:33
  67.6 11.7 %copy-start.23 = (f32[128,128]{1,0:T(8,128)S(1)}, f32[128,128]{1,0:T(8,128)}, u32[]{:S(2)}) copy-start(f32[128,128]{1,0:T(8,128)} %param.8) | copy-start | bytes 196612
  67.7 12.5 %copy-start.24 = (f32[128,128]{1,0:T(8,128)S(1)}, f32[128,128]{1,0:T(8,128)}, u32[]{:S(2)}) copy-start(f32[128,128]{1,0:T(8,128)} %param.10) | copy-start | bytes 196612
  68.8 31.9 %all-to-all-start.1 = ((f32[8,336,128]{2,1,0:T(8,128)}), f32[8,336,128]{2,1,0:T(8,128)S(1)}, u32[]{:S(2)}, u32[]{:S(2)}) async-start(f32[8,336,128]{2,1,0:T(8,128)} %broadcast_in_dim.12), calls=%async_computation.1 | async-start | bytes 2752512 | tf_op jit(solution)/shard_map/all_to_all | solution.py:53
  83.9 29.1 %collective-permute-start.2 = (f32[128,256]{0,1:T(8,128)}, f32[128,256]{0,1:T(8,128)}, u32[]{:S(2)}, u32[]{:S(2)}) collective-permute-start(f32[128,256]{0,1:T(8,128)} %slice_bitcast_fusion), channel_id=1, source_target_pairs={{0,0},{1,16},{2,32},{3,48},{4,64},{5,80},{6,96},{7,112},{8,8},{9,2... | collective-permute-start | bytes 393224 | tf_op jit(solution)/shard_map/ppermute | solution.py:155
  100.7 7.9 %copy-start.8 = (f32[8,336,128]{2,1,0:T(8,128)}, f32[8,336,128]{2,1,0:T(8,128)S(1)}, u32[]{:S(2)}) copy-start(f32[8,336,128]{2,1,0:T(8,128)S(1)} %all-to-all-done.1) | copy-start | bytes 4128772
  101.0 7.6 %copy-start.11 = (f32[1024,256]{1,0:T(8,128)S(1)}, f32[1024,256]{1,0:T(8,128)}, u32[]{:S(2)}) copy-start(f32[1024,256]{1,0:T(8,128)} %get-tuple-element.5) | copy-start | bytes 3145732
  101.0 7.6 %copy-start.18 = (f32[128,128]{0,1:T(8,128)S(1)}, f32[128,128]{0,1:T(8,128)}, u32[]{:S(2)}) copy-start(f32[128,128]{0,1:T(8,128)} %copy.19) | copy-start | bytes 196612
  101.0 7.6 %copy-start.20 = (f32[128,128]{0,1:T(8,128)S(1)}, f32[128,128]{0,1:T(8,128)}, u32[]{:S(2)}) copy-start(f32[128,128]{0,1:T(8,128)} %copy.20) | copy-start | bytes 196612
  103.1 19.6 %collective-permute-start.8 = (f32[512,128]{1,0:T(8,128)}, f32[512,128]{1,0:T(8,128)}, u32[]{:S(2)}, u32[]{:S(2)}) collective-permute-start(f32[512,128]{1,0:T(8,128)} %bitcast.14), channel_id=1, source_target_pairs={{0,8},{8,0},{16,24},{24,16},{32,40},{40,32},{48,56},{56,48},{64,72... | collective-permute-start | bytes 786440 | tf_op jit(solution)/shard_map/ppermute | solution.py:33
  106.1 26.3 %collective-permute-start.7 = (f32[8,256,128]{2,1,0:T(8,128)}, f32[8,256,128]{2,1,0:T(8,128)}, u32[]{:S(2)}, u32[]{:S(2)}) collective-permute-start(f32[8,256,128]{2,1,0:T(8,128)} %slice.35), channel_id=1, source_target_pairs={{0,8},{8,0},{16,24},{24,16},{32,40},{40,32},{48,56},{56,48},{64,72... | collective-permute-start | bytes 3145736 | tf_op jit(solution)/shard_map/ppermute | solution.py:33
  114.0 6.4 %copy-start.19 = (f32[128,128]{0,1:T(8,128)S(1)}, f32[128,128]{0,1:T(8,128)}, u32[]{:S(2)}) copy-start(f32[128,128]{0,1:T(8,128)} %copy.19) | copy-start | bytes 196612
  114.0 6.4 %copy-start.21 = (f32[128,128]{0,1:T(8,128)S(1)}, f32[128,128]{0,1:T(8,128)}, u32[]{:S(2)}) copy-start(f32[128,128]{0,1:T(8,128)} %copy.20) | copy-start | bytes 196612
  115.2 24.8 %all-to-all-start.2 = ((f32[8,160,256]{2,1,0:T(8,128)}), f32[8,160,256]{2,1,0:T(8,128)}, u32[]{:S(2)}, u32[]{:S(2)}) async-start(f32[8,160,256]{2,1,0:T(8,128)} %broadcast_in_dim.13), calls=%async_computation.2 | async-start | bytes 2621440 | tf_op jit(solution)/shard_map/all_to_all | solution.py:53
  128.0 4.4 %copy-start.9 = (f32[8,336,128]{2,1,0:T(8,128)S(1)}, f32[8,336,128]{2,1,0:T(8,128)}, u32[]{:S(2)}) copy-start(f32[8,336,128]{2,1,0:T(8,128)} %copy-done.8) | copy-start | bytes 4128772
  141.0 16.1 %collective-permute-start.5 = (f32[32,256]{1,0:T(8,128)S(1)}, f32[32,256]{1,0:T(8,128)S(1)}, u32[]{:S(2)}, u32[]{:S(2)}) collective-permute-start(f32[32,256]{1,0:T(8,128)S(1)} %slice_reduce_fusion), channel_id=1, source_target_pairs={{0,8},{8,0},{16,24},{24,16},{32,40},{40,32},{48,56},{56,48},{64,72... | collective-permute-start | bytes 98312 | tf_op jit(solution)/shard_map/ppermute | solution.py:33
  153.6 3.4 %copy-start.3 = (f32[1024,2048]{1,0:T(8,128)}, f32[1024,2048]{1,0:T(8,128)S(1)}, u32[]{:S(2)}) copy-start(f32[1024,2048]{1,0:T(8,128)S(1)} %shard_map.79.base_ref) | copy-start | bytes 25165828
  157.8 12.9 %all-to-all-start.3 = ((f32[8,32,256]{2,1,0:T(8,128)}), f32[8,32,256]{2,1,0:T(8,128)S(1)}, u32[]{:S(2)}, u32[]{:S(2)}) async-start(f32[8,32,256]{2,1,0:T(8,128)} %broadcast_in_dim.14), calls=%async_computation.3 | async-start | bytes 524288 | tf_op jit(solution)/shard_map/all_to_all | solution.py:53
  172.5 3.4 %copy-start.4 = (f32[1024,2048]{1,0:T(8,128)S(1)}, f32[1024,2048]{1,0:T(8,128)}, u32[]{:S(2)}) copy-start(f32[1024,2048]{1,0:T(8,128)} %copy-done.3) | copy-start | bytes 25165828
  (6 other events, 13.9 us)

commit v3 on v0

v3 whole, which is shorter than its diff:
```python
import jax
import jax.numpy as jnp
from jax import lax
from jax.experimental import pallas as pl
from jax.experimental.pallas import tpu as pltpu
from jax.sharding import PartitionSpec as P

HIGH = lax.Precision.HIGH
BOTH = ("row", "col")
SAME_CORE = [[2 * i + k for i in range(8)] for k in range(2)]
F32 = jnp.float32
BF16 = jnp.bfloat16
WIDE = 512


def dot(left, right, dims=((1,), (0,)), precision=HIGH):
    return lax.dot_general(left, right, (dims, ((), ())), precision=precision, preferred_element_type=F32)


def small(left, right, dims=((1,), (0,))):
    return dot(left, right, dims, lax.Precision.HIGHEST)


def split(value):
    high = value.astype(BF16)
    return high, (value - high.astype(F32)).astype(BF16)


def mxu(left, right):
    return jnp.dot(left, right, preferred_element_type=F32)


def three(left, right):
    left_high, left_low = split(left)
    right_high, right_low = split(right)
    return mxu(left_high, right_high) + mxu(left_low, right_high) + mxu(left_high, right_low)


def row_swap(value, mask):
    return lax.ppermute(value, "row", [(i, i ^ mask) for i in range(16)])


def turn_map():
    return [((2 * j + k) * 8 + c, (2 * c + k) * 8 + j) for j in range(8) for k in range(2) for c in range(8)]


def exchange(value, axis, groups):
    return lax.all_to_all(value, axis, 0, 0, axis_index_groups=groups, tiled=True)


def copies(value, times):
    return jnp.broadcast_to(value[None], (times,) + value.shape)


def params(mebibytes):
    return pltpu.CompilerParams(vmem_limit_bytes=mebibytes * 2**20)


def cost(flops, bytes_accessed):
    return pl.CostEstimate(flops=flops, bytes_accessed=bytes_accessed, transcendentals=0)


def chunk_products(both_ref, matrix_ref, out_ref):
    high, low = split(matrix_ref[...])
    first = mxu(both_ref[...], high)
    total = -(first[:256] + first[256:] + mxu(both_ref[:256], low))
    for side in range(total.shape[1] // 128):
        out_ref[side] = total[:, side * 128 : side * 128 + 128]


def away_kernel(which_ref, v1_ref, v2_ref, matrix_ref, out_ref, both_ref):
    @pl.when(pl.program_id(0) == 0)
    def _():
        high, low = split(v1_ref[...].T)
        both_ref[0:128] = high
        both_ref[256:384] = low
        high, low = split(v2_ref[...].T)
        both_ref[128:256] = high
        both_ref[384:512] = low

    chunk_products(both_ref, matrix_ref, out_ref)


def kept_kernel(which_ref, both_ref, matrix_ref, out_ref):
    chunk_products(both_ref, matrix_ref, out_ref)


def half_product(kernel, which, sides, side_specs, matrix, more_shapes, more_specs):
    depth = matrix.shape[0]
    return pl.pallas_call(
        kernel,
        grid_spec=pltpu.PrefetchScalarGridSpec(
            num_scalar_prefetch=1,
            grid=(1024 // WIDE,),
            in_specs=side_specs
            + [pl.BlockSpec((depth, WIDE), lambda i, which: (0, which[0] * (1024 // WIDE) + i))],
            out_specs=[pl.BlockSpec((WIDE // 128, 256, 128), lambda i, which: (i, 0, 0))] + more_specs,
        ),
        out_shape=[jax.ShapeDtypeStruct((8, 256, 128), F32)] + more_shapes,
        compiler_params=params(58),
        cost_estimate=cost(3 * 2 * 256 * depth * 1024, 4 * depth * 1024 + 2**21),
    )(which, *sides, matrix)


def away_product(which, v1, v2, matrix):
    depth = matrix.shape[0]
    return half_product(
        away_kernel,
        which,
        (v1, v2),
        [pl.BlockSpec((depth, 128), lambda i, which: (0, 0))] * 2,
        matrix,
        [jax.ShapeDtypeStruct((512, depth), BF16)],
        [pl.BlockSpec((512, depth), lambda i, which: (0, 0))],
    )


def kept_product(which, both, matrix):
    depth = matrix.shape[0]
    spec = pl.BlockSpec((512, depth), lambda i, which: (0, 0))
    return half_product(kept_kernel, which, (both,), [spec], matrix, [], [])[0]


def side_kernel(core_ref, both_ref, v2_ref, vectors_ref, away_ref, kept_ref, sums_ref):
    high, low = split(vectors_ref[...])
    sums_ref[...] = mxu(both_ref[:256], high) + mxu(both_ref[256:], high) + mxu(both_ref[:256], low)
    high, low = split(v2_ref[...])
    cross = mxu(both_ref[:128], high) + mxu(both_ref[256:384], high) + mxu(both_ref[:128], low)
    for out_ref, half in ((kept_ref, core_ref[0]), (away_ref, 1 - core_ref[0])):
        for j in range(8):
            rows = pl.ds(pl.multiple_of(half * 128 + j * 16, 16), 16)
            for block in range(4):
                out_ref[j, 16 * block : 16 * block + 16] = sums_ref[rows, block * 128 : block * 128 + 128]
            out_ref[j, 64:] = cross[j * 16 : j * 16 + 16]


def side_products(core, both, v2, vectors):
    return pl.pallas_call(
        side_kernel,
        in_specs=[pl.BlockSpec(memory_space=pltpu.SMEM)] + [pl.BlockSpec(memory_space=pltpu.VMEM)] * 3,
        out_shape=[jax.ShapeDtypeStruct((8, 80, 128), F32)] * 2,
        scratch_shapes=[pltpu.VMEM((256, 512), F32)],
        compiler_params=params(16),
        cost_estimate=cost(3 * 2 * 256 * 1024 * 640, 2**22),
    )(core, both, v2, vectors)


def pack_kernel(kept_ref, came_ref, side_kept_ref, side_came_ref, out_ref):
    out_ref[:, :256] = kept_ref[...] + came_ref[...]
    out_ref[:, 256:] = side_kept_ref[...] + side_came_ref[...]


def pack(*parts):
    return pl.pallas_call(
        pack_kernel,
        out_shape=jax.ShapeDtypeStruct((8, 336, 128), F32),
        compiler_params=params(16),
        cost_estimate=cost(2**19, 2**22),
    )(*parts)


def chunk_kernel(parts_ref, v_ref, out_ref, rows_ref):
    total = parts_ref[0]
    for j in range(1, 8):
        total = total + parts_ref[j]
    rows_ref[...] = total[:256].T
    gram = three(total[:256], v_ref[...])
    for j in range(8):
        out_ref[j, :336] = total
        out_ref[j, 336:368] = gram[j * 32 : j * 32 + 32, :128]
        out_ref[j, 368:400] = gram[j * 32 : j * 32 + 32, 128:]
        out_ref[j, 400:528] = v_ref[:, :128]
        out_ref[j, 528:] = v_ref[:, 128:]


def chunk_product(parts, v):
    return pl.pallas_call(
        chunk_kernel,
        out_shape=[jax.ShapeDtypeStruct((8, 656, 128), F32), jax.ShapeDtypeStruct((128, 256), F32)],
        compiler_params=params(16),
        cost_estimate=cost(3 * 2 * 256 * 256 * 128, 2**22),
    )(parts, v)


def rows_kernel(parts_ref, rows_ref, out_ref):
    total = parts_ref[0, 336:400]
    for j in range(1, 8):
        total = total + parts_ref[j, 336:400]
    for j in range(8):
        out_ref[j, :128] = rows_ref[...]
        out_ref[j, 128:, :128] = total[:32]
        out_ref[j, 128:, 128:] = total[32:]


def rows_pack(parts, rows):
    return pl.pallas_call(
        rows_kernel,
        out_shape=jax.ShapeDtypeStruct((8, 160, 256), F32),
        compiler_params=params(16),
        cost_estimate=cost(2**20, 2**22),
    )(parts, rows)


def turned_three(left, right):
    left_high, left_low = split(left)
    right_high, right_low = split(right)
    dims = (((1,), (1,)), ((), ()))
    return (
        lax.dot_general(left_high, right_high, dims, preferred_element_type=F32)
        + lax.dot_general(left_low, right_high, dims, preferred_element_type=F32)
        + lax.dot_general(left_high, right_low, dims, preferred_element_type=F32)
    )


def pick(core_ref, mine_ref, theirs_ref, run):
    own = pl.program_id(0) // (1024 // WIDE) == core_ref[0]

    @pl.when(own)
    def _():
        run(mine_ref)

    @pl.when(jnp.logical_not(own))
    def _():
        run(theirs_ref)


def first_kernel(core_ref, v1_ref, v2_ref, factor_ref, mine_ref, theirs_ref, base_ref, out_ref, y_ref, wide_ref):
    @pl.when(pl.program_id(0) == 0)
    def _():
        for j in range(4):
            rows = slice(j * 256, j * 256 + 256)
            y = turned_three(jnp.concatenate([v1_ref[rows], v2_ref[rows]], axis=1), factor_ref[...])
            y_ref[rows] = y
            high, low = split(y)
            wide_ref[rows, :256] = high
            wide_ref[rows, 256:] = low

    def run(chunks_ref):
        high, low = split(jnp.concatenate([chunks_ref[j, :256] for j in range(WIDE // 128)], axis=1))
        total = mxu(wide_ref[:, :256], high) + mxu(wide_ref[:, 256:], high) + mxu(wide_ref[:, :256], low)
        out_ref[...] = base_ref[...] + total

    pick(core_ref, mine_ref, theirs_ref, run)


def first_product(core, v1, v2, factor, mine, theirs, base):
    rows, cols = base.shape
    chunks = pl.BlockSpec((WIDE // 128, 656, 128), lambda i, core: (i % (1024 // WIDE), 0, 0))
    block = pl.BlockSpec((rows, WIDE), lambda i, core: (0, i))
    return pl.pallas_call(
        first_kernel,
        grid_spec=pltpu.PrefetchScalarGridSpec(
            num_scalar_prefetch=1,
            grid=(cols // WIDE,),
            in_specs=[pl.BlockSpec((rows, 128), lambda i, core: (0, 0))] * 2
            + [pl.BlockSpec((256, 256), lambda i, core: (0, 0)), chunks, chunks, block],
            out_specs=[block, pl.BlockSpec((rows, 256), lambda i, core: (0, 0))],
            scratch_shapes=[pltpu.VMEM((rows, 512), BF16)],
        ),
        out_shape=[jax.ShapeDtypeStruct((rows, cols), F32), jax.ShapeDtypeStruct((rows, 256), F32)],
        compiler_params=params(58),
        cost_estimate=cost(3 * 2 * rows * cols * 256, 8 * rows * cols),
    )(core, v1, v2, factor, mine, theirs, base)


def last_kernel(core_ref, y_ref, p_ref, gram_ref, factor_ref, mine_ref, theirs_ref, base_ref, out_ref, wide_ref):
    @pl.when(pl.program_id(0) == 0)
    def _():
        gram_high, gram_low = split(gram_ref[...].reshape(256, 256))
        for j in range(8):
            rows = slice(j * 128, j * 128 + 128)
            y_high, y_low = split(y_ref[rows])
            left = p_ref[j, :128] + (mxu(y_high, gram_high) + mxu(y_low, gram_high) + mxu(y_high, gram_low))
            high, low = split(left)
            wide_ref[rows, :256] = high
            wide_ref[rows, 256:] = low

    def run(chunks_ref):
        v = [
            jnp.concatenate([chunks_ref[j, 400:528], chunks_ref[j, 528:]], axis=1) for j in range(WIDE // 128)
        ]
        high, low = split(turned_three(factor_ref[...], jnp.concatenate(v, axis=0)))
        total = mxu(wide_ref[:, :256], high) + mxu(wide_ref[:, 256:], high) + mxu(wide_ref[:, :256], low)
        out_ref[...] = base_ref[...] - total

    pick(core_ref, mine_ref, theirs_ref, run)


def last_product(core, y, p, gram, factor, mine, theirs, base):
    rows, cols = base.shape
    chunks = pl.BlockSpec((WIDE // 128, 656, 128), lambda i, core: (i % (1024 // WIDE), 0, 0))
    block = pl.BlockSpec((rows, WIDE), lambda i, core: (0, i))
    return pl.pallas_call(
        last_kernel,
        grid_spec=pltpu.PrefetchScalarGridSpec(
            num_scalar_prefetch=1,
            grid=(cols // WIDE,),
            in_specs=[
                pl.BlockSpec((rows, 256), lambda i, core: (0, 0)),
                pl.BlockSpec((8, 160, 256), lambda i, core: (0, 0, 0)),
                pl.BlockSpec((8, 32, 256), lambda i, core: (0, 0, 0)),
                pl.BlockSpec((256, 256), lambda i, core: (0, 0)),
                chunks,
                chunks,
                block,
            ],
            out_specs=block,
            scratch_shapes=[pltpu.VMEM((rows, 512), BF16)],
        ),
        out_shape=jax.ShapeDtypeStruct((rows, cols), F32),
        compiler_params=params(58),
        cost_estimate=cost(3 * 2 * rows * cols * 256, 8 * rows * cols),
    )(core, y, p, gram, factor, mine, theirs, base)


def back_kernel(core_ref, v1_ref, v2_ref, factor_ref, mine_ref, theirs_ref, vectors_ref, out_ref, sums_ref):
    def place(ref, half):
        for j in range(8):
            for block in range(4):
                rows = slice(half * 128 + j * 16, half * 128 + j * 16 + 16)
                sums_ref[rows, block * 128 : block * 128 + 128] = ref[j, 256 + 16 * block : 272 + 16 * block]

    @pl.when(core_ref[0] == 0)
    def _():
        place(mine_ref, 0)
        place(theirs_ref, 1)

    @pl.when(core_ref[0] == 1)
    def _():
        place(mine_ref, 1)
        place(theirs_ref, 0)

    mixed = three(factor_ref[...], sums_ref[...])
    out_ref[...] = vectors_ref[...] - three(v1_ref[...], mixed[:128]) - three(v2_ref[...], mixed[128:])


def back_product(core, v1, v2, factor, mine, theirs, vectors):
    return pl.pallas_call(
        back_kernel,
        in_specs=[pl.BlockSpec(memory_space=pltpu.SMEM)] + [pl.BlockSpec(memory_space=pltpu.VMEM)] * 6,
        out_shape=jax.ShapeDtypeStruct(vectors.shape, F32),
        scratch_shapes=[pltpu.VMEM((256, 512), F32)],
        compiler_params=params(16),
        cost_estimate=cost(3 * 2 * 1280 * 256 * 512, 2**23),
    )(core, v1, v2, factor, mine, theirs, vectors)


def shards(matrix, v1, f1, v2, f2, vectors):
    core = lax.axis_index("row") % 2
    col = lax.axis_index("col")

    v_chunk = jnp.concatenate(
        [lax.dynamic_slice_in_dim(v1, col * 128, 128, 0), lax.dynamic_slice_in_dim(v2, col * 128, 128, 0)], axis=1
    )
    v_chunk = lax.ppermute(v_chunk, BOTH, turn_map())

    away, both = away_product((1 - core)[None], v1, v2, matrix)
    came = row_swap(away, 1)
    side_away, side_kept = side_products(core[None], both, v2, vectors)
    side_came = row_swap(side_away, 1)
    kept = kept_product(core[None], both, matrix)

    packed = pack(kept, came, side_kept, side_came)
    packed, v_chunk = lax.optimization_barrier((packed, v_chunk))
    parts = exchange(packed, "row", SAME_CORE)

    packed, over = chunk_product(parts, v_chunk)
    got = exchange(packed, "row", SAME_CORE)
    over = lax.ppermute(over, BOTH, turn_map())
    got, over = lax.optimization_barrier((got, over))

    p_rows = exchange(rows_pack(got, over), "col", None)

    theirs = row_swap(got, 1)
    cross = got[:, 320:336].reshape(128, 128)
    a_right = -small(small(f1, cross), f2)
    factor = jnp.concatenate(
        [jnp.concatenate([f1, a_right], axis=1), jnp.concatenate([jnp.zeros_like(f2), f2], axis=1)], axis=0
    )
    back = back_product(core[None], v1, v2, factor, got, theirs, vectors)
    inner, y_rows = first_product(core[None], v1, v2, factor, got, theirs, matrix)
    p_rows, inner, back = lax.optimization_barrier((p_rows, inner, back))

    gram = p_rows[:, 128:].sum(0)
    gram = gram + row_swap(gram, 1)
    gram = exchange(copies(gram, 8), "row", SAME_CORE)

    updated = last_product(core[None], y_rows, p_rows, gram, factor, got, theirs, inner)
    return updated, back


def solution(mesh):
    in_specs = (P("row", "col"), P("row", None), P(), P("row", None), P(), P("row", "col"))
    out_specs = (P("row", "col"), P("row", "col"))
    return jax.shard_map(shards, mesh=mesh, in_specs=in_specs, out_specs=out_specs, check_vma=False)
```

time: 678 us -> 151 us (0.22)
  waiting for transfers between devices: 533 us -> 36.4 us
  matrix products: 114 us -> 0.57 us
  Pallas kernels: 0 us -> 43.4 us
  blocking collectives: 0 us -> 42.8 us
  starting transfers between devices: 1.09 us -> 16.6 us
  between operations: 14.5 us -> 0.86 us
    psum x4 -> x0, waiting for transfers between devices: 378 us -> none  [the longest x2 283 us: transform(): summed_cols = lax.psum(partial_cols, 'row')]
    all_gather x2 -> x0, waiting for transfers between devices: 154 us -> none  [the longest x1 78.8 us: shards(): lax.all_gather(first_reflector, 'row', axis=0, tiled=True)]
    dot_general x26 -> x2, matrix products: 114 us -> 0.57 us  [dot(): lax.dot_general(left, right, (dims, ((), ())), precision=precision, prefe...]
    pallas_call x0 -> x9, Pallas kernels: none -> 43.4 us  [the longest x1 13.7 us: last_product(): pl.pallas_call(last_kernel, grid_spec=pltpu.PrefetchScalarGridSpec(num_sc...]
    all_to_all x0 -> x2, blocking collectives: none -> 42.8 us  [exchange(): lax.all_to_all(value, axis, 0, 0, axis_index_groups=groups, tiled=True)]
    all_to_all x0 -> x2, waiting for transfers between devices: none -> 35.5 us  [exchange(): lax.all_to_all(value, axis, 0, 0, axis_index_groups=groups, tiled=True)]
    all_to_all x0 -> x2, starting transfers between devices: none -> 9.16 us  [exchange(): lax.all_to_all(value, axis, 0, 0, axis_index_groups=groups, tiled=True)]
    ppermute x0 -> x6, starting transfers between devices: none -> 7.42 us  [the longest x4 6.09 us: row_swap(): return lax.ppermute(value, 'row', [(i, i ^ mask) for i in range(16)])]
  transfers between devices with their start and end apart: 6 -> 8, of which waited for: 6 -> 2; matrix products, arithmetic and copies ran while one was open for 8% -> 0% of each run, Pallas kernels for 0% -> 16%
where the time goes in v3:
time: 151 us; the launch traced here: 149 us
  Pallas kernels  43.4 us (29%)
  blocking collectives  42.8 us (28%)
  waiting for transfers between devices  36.4 us (24%)
  starting transfers between devices  16.6 us (11%)
  local copies, waits for them, and re-layouts  7.79 us (5%)
    all_to_all x2, blocking collectives, exchange(): lax.all_to_all(value, axis, 0, 0, axis_index_groups=groups, tiled=True)  42.8 us
    all_to_all x2, waiting for transfers between devices, exchange(): lax.all_to_all(value, axis, 0, 0, axis_index_groups=groups, tiled=True)  35.5 us
    pallas_call x1, Pallas kernels, last_product(): pl.pallas_call(last_kernel, grid_spec=pltpu.PrefetchScalarGridSpec(num_sc...  13.7 us
    pallas_call x1, Pallas kernels, first_product(): pl.pallas_call(first_kernel, grid_spec=pltpu.PrefetchScalarGridSpec(num_s...  12.9 us
    pallas_call x2, Pallas kernels, half_product(): pl.pallas_call(kernel, grid_spec=pltpu.PrefetchScalarGridSpec(num_scalar_...  9.86 us
    all_to_all x2, starting transfers between devices, exchange(): lax.all_to_all(value, axis, 0, 0, axis_index_groups=groups, tiled=True)  9.16 us
    unnamed x26, local copies, waits for them, and re-layouts  7.74 us
    ppermute x4, starting transfers between devices, row_swap(): return lax.ppermute(value, 'row', [(i, i ^ mask) for i in range(16)])  6.09 us
  transfers between devices with their start and end apart: 8, of which 2 were waited for; matrix products, arithmetic and copies ran while one was open for 0% of the time, Pallas kernels for 16%

profile of v3, /device:TPU:1, one launch (start us, length us, event | category | flops | bytes accessed | tf_op | source)
XLA Modules:
  0.0 149.4 jit_solution(7718315333159264252)
XLA Ops:
  0.6 0.0 copy-start.3
  0.7 0.0 copy-start.8
  0.7 5.2 %shard_map.77 = (f32[8,256,128]{2,1,0:T(8,128)}, bf16[512,1024]{1,0:T(8,128)(2,1)}) custom-call(s32[1]{0:T(128)} %bitcast.1.which_ref, f32[1024,128]{1,0:T(8,128)} %v1_ref.5, f32[1024,128]{1,0:T(8,128)} %v2_ref.7, f32[1024,2048]{1,0:T(8,128)} %base_ref.1), custom_call_target="tpu_custom_call" | custom-call | flops 1610612736 | bytes 6291456 | tf_op jit(solution)/shard_map/pallas_call | solution.py:90
  5.8 1.4 collective-permute-start
  7.3 1.2 copy-done.10
  8.5 1.2 shard_map.79
  9.7 0.2 collective-permute-start.1
  9.9 0.7 collective-permute-start.2
  10.6 4.7 %shard_map.78.kept_ref = f32[8,256,128]{2,1,0:T(8,128)} custom-call(s32[1]{0:T(128)} %bitcast.which_ref.core_ref, bf16[512,1024]{1,0:T(8,128)(2,1)} %get-tuple-element.17.both_ref, f32[1024,2048]{1,0:T(8,128)} %base_ref.1), custom_call_target="tpu_custom_call" | custom-call | flops 1610612736 | bytes 6291456 | tf_op jit(solution)/shard_map/pallas_call | solution.py:90
  15.3 1.2 copy-done.6
  16.5 0.1 shard_map.80
  16.7 32.0 %all_to_all.20.parts_ref = f32[8,336,128]{2,1,0:T(8,128)S(1)} all-to-all(f32[8,336,128]{2,1,0:T(8,128)S(1)} %shard_map.80), channel_id=1, replica_groups={{0,16,32,48,64,80,96,112},{8,24,40,56,72,88,104,120},{1,17,33,49,65,81,..., dimensions={0} | all-to-all | bytes 2752512 | tf_op jit(solution)/shard_map/all_to_all | solution.py:48
  48.7 0.3 shard_map.81
  49.1 1.5 %copy-done.7 = f32[8,656,128]{2,1,0:T(8,128)} copy-done((f32[8,656,128]{2,1,0:T(8,128)}, f32[8,656,128]{2,1,0:T(8,128)S(1)}, u32[]{:S(2)}) %copy-start.7) | copy-done | bytes 2687000
  50.6 3.6 %all-to-all-start.1 = ((f32[8,656,128]{2,1,0:T(8,128)}), f32[8,656,128]{2,1,0:T(8,128)S(1)}, u32[]{:S(2)}, u32[]{:S(2)}) async-start(f32[8,656,128]{2,1,0:T(8,128)} %copy-done.7), calls=%async_computation.1 | async-start | bytes 5373952 | tf_op jit(solution)/shard_map/all_to_all | solution.py:48
  54.2 0.7 collective-permute-start.3
  54.9 35.5 %all-to-all-done.1.mine_ref.parts_ref = f32[8,656,128]{2,1,0:T(8,128)S(1)} async-done(((f32[8,656,128]{2,1,0:T(8,128)}), f32[8,656,128]{2,1,0:T(8,128)S(1)}, u32[]{:S(2)}, u32[]{:S(2)}) %all-to-all-start.1) | async-done | bytes 2687008 | tf_op jit(solution)/shard_map/all_to_all | solution.py:48
  90.4 4.1 %collective-permute-start.4 = (f32[8,656,128]{2,1,0:T(8,128)S(1)}, f32[8,656,128]{2,1,0:T(8,128)}, u32[]{:S(2)}, u32[]{:S(2)}) collective-permute-start(f32[8,656,128]{2,1,0:T(8,128)S(1)} %all-to-all-done.1.mine_ref.parts_ref), channel_id=1, source_target_pairs={{0,8},{8,0},{16,24},{24,16},{32,40},{40,32},{48,56},{56,48},{64,72... | collective-permute-start | bytes 8060936 | tf_op jit(solution)/shard_map/ppermute | solution.py:40
  94.5 0.1 shard_map.83
  94.6 1.0 copy-done.1
  95.7 5.5 %all-to-all-start.2 = ((f32[8,160,256]{2,1,0:T(8,128)}), f32[8,160,256]{2,1,0:T(8,128)}, u32[]{:S(2)}, u32[]{:S(2)}) async-start(f32[8,160,256]{2,1,0:T(8,128)} %copy-done.1), calls=%async_computation.2 | async-start | bytes 2621440 | tf_op jit(solution)/shard_map/all_to_all | solution.py:48
  101.2 0.3 fusion
  101.5 0.3 convolution_negate_fusion
  101.9 1.1 copy-done.4
  103.0 1.6 %copy-done.9 = f32[1024,512]{1,0:T(8,128)S(1)} copy-done((f32[1024,512]{1,0:T(8,128)S(1)}, f32[1024,512]{1,0:T(8,128)}, u32[]{:S(2)}) %copy-start.9) | copy-done | bytes 2097176
  104.6 5.2 %shard_map.84 = f32[1024,512]{1,0:T(8,128)} custom-call(s32[1]{0:T(128)} %bitcast.which_ref.core_ref, f32[1024,128]{1,0:T(8,128)S(1)} %copy-done.2, f32[1024,128]{1,0:T(8,128)S(1)} %copy-done.4, f32[256,256]{1,0:T(8,128)S(1)} %select_maximum_fusion.factor_ref, f32[8,656,128]{2,1,0:T(8,128)S(1)} %all-to-all-done.1.mine_ref.parts_ref, ...), custom_call_target="tpu_custom_call" | custom-call | flops 1006632960 | bytes 8388608 | tf_op jit(solution)/shard_map/pallas_call | solution.py:338
  109.8 12.9 %shard_map.82 = (f32[1024,2048]{1,0:T(8,128)}, f32[1024,256]{1,0:T(8,128)}) custom-call(s32[1]{0:T(128)} %bitcast.which_ref.core_ref, f32[1024,128]{1,0:T(8,128)} %v1_ref.5, f32[1024,128]{1,0:T(8,128)} %v2_ref.7, f32[256,256]{1,0:T(8,128)} %copy-done.5, f32[8,656,128]{2,1,0:T(8,128)} %copy-done, f32[8,656,128]{2,1,0:T(8,128)} %collective-permute-done.4.theirs_ref, ...), custom_call_target="tpu_custom_call" | custom-call | flops 3221225472 | bytes 16777216 | tf_op jit(solution)/shard_map/pallas_call | solution.py:250
  122.7 1.0 slice_reduce_fusion
  123.7 0.4 collective-permute-start.5
  124.1 0.9 collective-permute-done.5
  125.0 10.7 %all_to_all.21.gram_ref = f32[8,32,256]{2,1,0:T(8,128)} all-to-all(f32[8,32,256]{2,1,0:T(8,128)S(1)} %broadcast_in_dim.8), channel_id=1, replica_groups={{0,16,32,48,64,80,96,112},{8,24,40,56,72,88,104,120},{1,17,33,49,65,81,..., dimensions={0} | all-to-all | bytes 524288 | tf_op jit(solution)/shard_map/all_to_all | solution.py:48
  135.8 13.7 %shard_map.85 = f32[1024,2048]{1,0:T(8,128)} custom-call(s32[1]{0:T(128)} %bitcast.which_ref.core_ref, f32[1024,256]{1,0:T(8,128)} %get-tuple-element.26.y_ref, f32[8,160,256]{2,1,0:T(8,128)} %all-to-all-done.2.p_ref, f32[8,32,256]{2,1,0:T(8,128)} %all_to_all.21.gram_ref, f32[256,256]{1,0:T(8,128)} %copy-done.5, f32[8,656,128]{2,1,0:T(8,128)} %copy-done, ...), custom_call_target="tpu_custom_call" | custom-call | flops 3221225472 | bytes 16777216 | tf_op jit(solution)/shard_map/pallas_call | solution.py:293
  (31 shorter events, 0.1 us)
Async XLA Ops:
  0.6 6.6 %copy-start.3 = (f32[1024,128]{1,0:T(8,128)S(1)}, f32[1024,128]{1,0:T(8,128)}, u32[]{:S(2)}) copy-start(f32[1024,128]{1,0:T(8,128)} %v2_ref.7) | copy-start | bytes 1572868
  0.7 6.6 %copy-start.8 = (f32[1024,512]{1,0:T(8,128)S(1)}, f32[1024,512]{1,0:T(8,128)}, u32[]{:S(2)}) copy-start(f32[1024,512]{1,0:T(8,128)} %vectors_ref.3) | copy-start | bytes 6291460
  5.8 4.1 %copy-start.2 = (f32[1024,128]{1,0:T(8,128)S(1)}, f32[1024,128]{1,0:T(8,128)}, u32[]{:S(2)}) copy-start(f32[1024,128]{1,0:T(8,128)} %v1_ref.5) | copy-start | bytes 1572868
  5.8 9.5 %collective-permute-start = (f32[8,256,128]{2,1,0:T(8,128)}, f32[8,256,128]{2,1,0:T(8,128)S(1)}, u32[]{:S(2)}, u32[]{:S(2)}) collective-permute-start(f32[8,256,128]{2,1,0:T(8,128)} %get-tuple-element.18), channel_id=1, source_target_pairs={{0,8},{8,0},{16,24},{24,16},{32,40},{40,32},{48,56},{56,48},{64,72... | collective-permute-start | bytes 3145736 | tf_op jit(solution)/shard_map/ppermute | solution.py:40
  7.3 1.2 copy-start.10
  9.7 5.6 %collective-permute-start.1 = (f32[8,80,128]{2,1,0:T(8,128)S(1)}, f32[8,80,128]{2,1,0:T(8,128)S(1)}, u32[]{:S(2)}, u32[]{:S(2)}) collective-permute-start(f32[8,80,128]{2,1,0:T(8,128)S(1)} %get-tuple-element.20), channel_id=1, source_target_pairs={{0,8},{8,0},{16,24},{24,16},{32,40},{40,32},{48,56},{56,48},{64,72... | collective-permute-start | bytes 983048 | tf_op jit(solution)/shard_map/ppermute | solution.py:40
  9.9 6.8 %collective-permute-start.2 = (f32[128,256]{1,0:T(8,128)S(1)}, f32[128,256]{1,0:T(8,128)S(1)}, u32[]{:S(2)}, u32[]{:S(2)}) collective-permute-start(f32[128,256]{1,0:T(8,128)S(1)} %pad_maximum_fusion), channel_id=1, source_target_pairs={{0,0},{1,16},{2,32},{3,48},{4,64},{5,80},{6,96},{7,112},{8,8},{9,2... | collective-permute-start | bytes 393224 | tf_op jit(solution)/shard_map/ppermute | solution.py:355
  15.3 1.2 copy-start.6
  49.0 1.5 %copy-start.7 = (f32[8,656,128]{2,1,0:T(8,128)}, f32[8,656,128]{2,1,0:T(8,128)S(1)}, u32[]{:S(2)}) copy-start(f32[8,656,128]{2,1,0:T(8,128)S(1)} %get-tuple-element.23) | copy-start | bytes 8060932
  50.6 39.9 %all-to-all-start.1 = ((f32[8,656,128]{2,1,0:T(8,128)}), f32[8,656,128]{2,1,0:T(8,128)S(1)}, u32[]{:S(2)}, u32[]{:S(2)}) async-start(f32[8,656,128]{2,1,0:T(8,128)} %copy-done.7), calls=%async_computation.1 | async-start | bytes 5373952 | tf_op jit(solution)/shard_map/all_to_all | solution.py:48
  54.2 0.7 collective-permute-start.3
  90.4 11.4 %copy-start = (f32[8,656,128]{2,1,0:T(8,128)}, f32[8,656,128]{2,1,0:T(8,128)S(1)}, u32[]{:S(2)}) copy-start(f32[8,656,128]{2,1,0:T(8,128)S(1)} %all-to-all-done.1.mine_ref.parts_ref) | copy-start | bytes 8060932
  90.4 11.4 %collective-permute-start.4 = (f32[8,656,128]{2,1,0:T(8,128)S(1)}, f32[8,656,128]{2,1,0:T(8,128)}, u32[]{:S(2)}, u32[]{:S(2)}) collective-permute-start(f32[8,656,128]{2,1,0:T(8,128)S(1)} %all-to-all-done.1.mine_ref.parts_ref), channel_id=1, source_target_pairs={{0,8},{8,0},{16,24},{24,16},{32,40},{40,32},{48,56},{56,48},{64,72... | collective-permute-start | bytes 8060936 | tf_op jit(solution)/shard_map/ppermute | solution.py:40
  94.6 1.1 copy-start.1
  95.7 5.5 %copy-start.12 = (f32[128,128]{1,0:T(8,128)S(1)}, f32[128,128]{1,0:T(8,128)}, u32[]{:S(2)}) copy-start(f32[128,128]{1,0:T(8,128)} %param.8) | copy-start | bytes 196612
  95.7 5.8 %copy-start.11 = (f32[128,128]{1,0:T(8,128)S(1)}, f32[128,128]{1,0:T(8,128)}, u32[]{:S(2)}) copy-start(f32[128,128]{1,0:T(8,128)} %param.10) | copy-start | bytes 196612
  95.7 27.1 %all-to-all-start.2 = ((f32[8,160,256]{2,1,0:T(8,128)}), f32[8,160,256]{2,1,0:T(8,128)}, u32[]{:S(2)}, u32[]{:S(2)}) async-start(f32[8,160,256]{2,1,0:T(8,128)} %copy-done.1), calls=%async_computation.2 | async-start | bytes 2621440 | tf_op jit(solution)/shard_map/all_to_all | solution.py:48
  101.8 8.0 %copy-start.5 = (f32[256,256]{1,0:T(8,128)}, f32[256,256]{1,0:T(8,128)S(1)}, u32[]{:S(2)}) copy-start(f32[256,256]{1,0:T(8,128)S(1)} %select_maximum_fusion.factor_ref) | copy-start | bytes 786436
  101.9 1.1 copy-start.4
  103.0 1.6 %copy-start.9 = (f32[1024,512]{1,0:T(8,128)S(1)}, f32[1024,512]{1,0:T(8,128)}, u32[]{:S(2)}) copy-start(f32[1024,512]{1,0:T(8,128)} %vectors_ref.3) | copy-start | bytes 6291460
  123.7 1.3 collective-permute-start.5

commit v4 on v3

--- a/solution.py
+++ b/solution.py
@@ -166,11 +166,13 @@
     rows_ref[...] = total[:256].T
     gram = three(total[:256], v_ref[...])
     for j in range(8):
-        out_ref[j, :336] = total
-        out_ref[j, 336:368] = gram[j * 32 : j * 32 + 32, :128]
-        out_ref[j, 368:400] = gram[j * 32 : j * 32 + 32, 128:]
-        out_ref[j, 400:528] = v_ref[:, :128]
-        out_ref[j, 528:] = v_ref[:, 128:]
+        out_ref[j, :256] = total[:256]
+        out_ref[j, 256:384] = v_ref[:, :128]
+        out_ref[j, 384:512] = v_ref[:, 128:]
+        out_ref[j, 512:576] = total[256:320]
+        out_ref[j, 576:608] = gram[j * 32 : j * 32 + 32, :128]
+        out_ref[j, 608:640] = gram[j * 32 : j * 32 + 32, 128:]
+        out_ref[j, 640:] = total[320:]
 
 
 def chunk_product(parts, v):
@@ -183,9 +185,9 @@
 
 
 def rows_kernel(parts_ref, rows_ref, out_ref):
-    total = parts_ref[0, 336:400]
+    total = parts_ref[0]
     for j in range(1, 8):
-        total = total + parts_ref[j, 336:400]
+        total = total + parts_ref[j]
     for j in range(8):
         out_ref[j, :128] = rows_ref[...]
         out_ref[j, 128:, :128] = total[:32]
@@ -195,6 +197,9 @@
 def rows_pack(parts, rows):
     return pl.pallas_call(
         rows_kernel,
+        grid=(1,),
+        in_specs=[pl.BlockSpec((8, 64, 128), lambda i: (0, 9, 0)), pl.BlockSpec((128, 256), lambda i: (0, 0))],
+        out_specs=pl.BlockSpec((8, 160, 256), lambda i: (0, 0, 0)),
         out_shape=jax.ShapeDtypeStruct((8, 160, 256), F32),
         compiler_params=params(16),
         cost_estimate=cost(2**20, 2**22),
@@ -212,8 +217,8 @@
     )
 
 
-def pick(core_ref, mine_ref, theirs_ref, run):
-    own = pl.program_id(0) // (1024 // WIDE) == core_ref[0]
+def pick(mine_ref, theirs_ref, run):
+    own = pl.program_id(0) < 1024 // WIDE
 
     @pl.when(own)
     def _():
@@ -222,6 +227,15 @@
     @pl.when(jnp.logical_not(own))
     def _():
         run(theirs_ref)
+
+
+def half_specs(rows, part):
+    steps = 1024 // WIDE
+    return (
+        pl.BlockSpec((rows, WIDE), lambda i, core: (0, (core[0] * steps + i) % (2 * steps))),
+        pl.BlockSpec((WIDE // 128, 256, 128), lambda i, core: (jnp.minimum(i, steps - 1), part, 0)),
+        pl.BlockSpec((WIDE // 128, 256, 128), lambda i, core: (jnp.maximum(i - steps, 0), part, 0)),
+    )
 
 
 def first_kernel(core_ref, v1_ref, v2_ref, factor_ref, mine_ref, theirs_ref, base_ref, out_ref, y_ref, wide_ref):
@@ -236,24 +250,23 @@
             wide_ref[rows, 256:] = low
 
     def run(chunks_ref):
-        high, low = split(jnp.concatenate([chunks_ref[j, :256] for j in range(WIDE // 128)], axis=1))
+        high, low = split(jnp.concatenate([chunks_ref[j] for j in range(WIDE // 128)], axis=1))
         total = mxu(wide_ref[:, :256], high) + mxu(wide_ref[:, 256:], high) + mxu(wide_ref[:, :256], low)
         out_ref[...] = base_ref[...] + total
 
-    pick(core_ref, mine_ref, theirs_ref, run)
+    pick(mine_ref, theirs_ref, run)
 
 
 def first_product(core, v1, v2, factor, mine, theirs, base):
     rows, cols = base.shape
-    chunks = pl.BlockSpec((WIDE // 128, 656, 128), lambda i, core: (i % (1024 // WIDE), 0, 0))
-    block = pl.BlockSpec((rows, WIDE), lambda i, core: (0, i))
+    block, mine_part, theirs_part = half_specs(rows, 0)
     return pl.pallas_call(
         first_kernel,
         grid_spec=pltpu.PrefetchScalarGridSpec(
             num_scalar_prefetch=1,
             grid=(cols // WIDE,),
             in_specs=[pl.BlockSpec((rows, 128), lambda i, core: (0, 0))] * 2
-            + [pl.BlockSpec((256, 256), lambda i, core: (0, 0)), chunks, chunks, block],
+            + [pl.BlockSpec((256, 256), lambda i, core: (0, 0)), mine_part, theirs_part, block],
             out_specs=[block, pl.BlockSpec((rows, 256), lambda i, core: (0, 0))],
             scratch_shapes=[pltpu.VMEM((rows, 512), BF16)],
         ),
@@ -277,19 +290,18 @@
 
     def run(chunks_ref):
         v = [
-            jnp.concatenate([chunks_ref[j, 400:528], chunks_ref[j, 528:]], axis=1) for j in range(WIDE // 128)
+            jnp.concatenate([chunks_ref[j, :128], chunks_ref[j, 128:]], axis=1) for j in range(WIDE // 128)
         ]
         high, low = split(turned_three(factor_ref[...], jnp.concatenate(v, axis=0)))
         total = mxu(wide_ref[:, :256], high) + mxu(wide_ref[:, 256:], high) + mxu(wide_ref[:, :256], low)
         out_ref[...] = base_ref[...] - total
 
-    pick(core_ref, mine_ref, theirs_ref, run)
+    pick(mine_ref, theirs_ref, run)
 
 
 def last_product(core, y, p, gram, factor, mine, theirs, base):
     rows, cols = base.shape
-    chunks = pl.BlockSpec((WIDE // 128, 656, 128), lambda i, core: (i % (1024 // WIDE), 0, 0))
-    block = pl.BlockSpec((rows, WIDE), lambda i, core: (0, i))
+    block, mine_part, theirs_part = half_specs(rows, 1)
     return pl.pallas_call(
         last_kernel,
         grid_spec=pltpu.PrefetchScalarGridSpec(
@@ -300,8 +312,8 @@
                 pl.BlockSpec((8, 160, 256), lambda i, core: (0, 0, 0)),
                 pl.BlockSpec((8, 32, 256), lambda i, core: (0, 0, 0)),
                 pl.BlockSpec((256, 256), lambda i, core: (0, 0)),
-                chunks,
-                chunks,
+                mine_part,
+                theirs_part,
                 block,
             ],
             out_specs=block,
@@ -318,7 +330,7 @@
         for j in range(8):
             for block in range(4):
                 rows = slice(half * 128 + j * 16, half * 128 + j * 16 + 16)
-                sums_ref[rows, block * 128 : block * 128 + 128] = ref[j, 256 + 16 * block : 272 + 16 * block]
+                sums_ref[rows, block * 128 : block * 128 + 128] = ref[j, 16 * block : 16 * block + 16]
 
     @pl.when(core_ref[0] == 0)
     def _():
@@ -335,12 +347,20 @@
 
 
 def back_product(core, v1, v2, factor, mine, theirs, vectors):
+    rows = vectors.shape[0]
+    whole = lambda height, width: pl.BlockSpec((height, width), lambda i, core: (0, 0))
+    part = pl.BlockSpec((8, 64, 128), lambda i, core: (0, 8, 0))
     return pl.pallas_call(
         back_kernel,
-        in_specs=[pl.BlockSpec(memory_space=pltpu.SMEM)] + [pl.BlockSpec(memory_space=pltpu.VMEM)] * 6,
+        grid_spec=pltpu.PrefetchScalarGridSpec(
+            num_scalar_prefetch=1,
+            grid=(1,),
+            in_specs=[whole(rows, 128), whole(rows, 128), whole(256, 256), part, part, whole(rows, 512)],
+            out_specs=whole(rows, 512),
+            scratch_shapes=[pltpu.VMEM((256, 512), F32)],
+        ),
         out_shape=jax.ShapeDtypeStruct(vectors.shape, F32),
-        scratch_shapes=[pltpu.VMEM((256, 512), F32)],
-        compiler_params=params(16),
+        compiler_params=params(24),
         cost_estimate=cost(3 * 2 * 1280 * 256 * 512, 2**23),
     )(core, v1, v2, factor, mine, theirs, vectors)
 
@@ -372,19 +392,20 @@
     p_rows = exchange(rows_pack(got, over), "col", None)
 
     theirs = row_swap(got, 1)
-    cross = got[:, 320:336].reshape(128, 128)
+    cross = got[:, 640:].reshape(128, 128)
     a_right = -small(small(f1, cross), f2)
     factor = jnp.concatenate(
         [jnp.concatenate([f1, a_right], axis=1), jnp.concatenate([jnp.zeros_like(f2), f2], axis=1)], axis=0
     )
     back = back_product(core[None], v1, v2, factor, got, theirs, vectors)
     inner, y_rows = first_product(core[None], v1, v2, factor, got, theirs, matrix)
-    p_rows, inner, back = lax.optimization_barrier((p_rows, inner, back))
+    p_rows, inner = lax.optimization_barrier((p_rows, inner))
 
     gram = p_rows[:, 128:].sum(0)
     gram = gram + row_swap(gram, 1)
     gram = exchange(copies(gram, 8), "row", SAME_CORE)
 
+    gram, back = lax.optimization_barrier((gram, back))
     updated = last_product(core[None], y_rows, p_rows, gram, factor, got, theirs, inner)
     return updated, back
 

time: 151 us -> 151 us (level)
  blocking collectives: 42.8 us -> 32.1 us
  waiting for transfers between devices: 36.4 us -> 45.4 us
  starting transfers between devices: 16.6 us -> 21.4 us
  Pallas kernels: 43.4 us -> 38.7 us
    all_to_all x2 -> x1, blocking collectives: 42.8 us -> 32.1 us  [exchange(): lax.all_to_all(value, axis, 0, 0, axis_index_groups=groups, tiled=True)]
    all_to_all x2 -> x3, waiting for transfers between devices: 35.5 us -> 44.5 us  [exchange(): lax.all_to_all(value, axis, 0, 0, axis_index_groups=groups, tiled=True)]
    all_to_all x2 -> x3, starting transfers between devices: 9.16 us -> 13.2 us  [exchange(): lax.all_to_all(value, axis, 0, 0, axis_index_groups=groups, tiled=True)]
    pallas_call x1, Pallas kernels: 13.7 us -> 11.5 us  [last_product(): pl.pallas_call(last_kernel, grid_spec=pltpu.PrefetchScalarGridSpec(num_sc...]
    pallas_call x1, Pallas kernels: 12.9 us -> 10.9 us  [first_product(): pl.pallas_call(first_kernel, grid_spec=pltpu.PrefetchScalarGridSpec(num_s...]
    unnamed x26 -> x28, local copies, waits for them, and re-layouts: 7.74 us -> 7.66 us
  transfers between devices with their start and end apart: 8 -> 9, of which waited for: 2 -> 4; matrix products, arithmetic and copies ran while one was open for 0% -> 1% of each run, Pallas kernels for 16% -> 14%
where the time goes in v4:
time: 151 us; the launch traced here: 150 us
  waiting for transfers between devices  45.4 us (30%)
  Pallas kernels  38.7 us (26%)
  blocking collectives  32.1 us (21%)
  starting transfers between devices  21.4 us (14%)
  local copies, waits for them, and re-layouts  9.25 us (6%)
  other arithmetic  1.71 us (1%)
    all_to_all x3, waiting for transfers between devices, exchange(): lax.all_to_all(value, axis, 0, 0, axis_index_groups=groups, tiled=True)  44.5 us
    all_to_all x1, blocking collectives, exchange(): lax.all_to_all(value, axis, 0, 0, axis_index_groups=groups, tiled=True)  32.1 us
    all_to_all x3, starting transfers between devices, exchange(): lax.all_to_all(value, axis, 0, 0, axis_index_groups=groups, tiled=True)  13.2 us
    pallas_call x1, Pallas kernels, last_product(): pl.pallas_call(last_kernel, grid_spec=pltpu.PrefetchScalarGridSpec(num_sc...  11.5 us
    pallas_call x1, Pallas kernels, first_product(): pl.pallas_call(first_kernel, grid_spec=pltpu.PrefetchScalarGridSpec(num_s...  10.9 us
    pallas_call x2, Pallas kernels, half_product(): pl.pallas_call(kernel, grid_spec=pltpu.PrefetchScalarGridSpec(num_scalar_...  9.85 us
    unnamed x28, local copies, waits for them, and re-layouts  7.66 us
    ppermute x4, starting transfers between devices, row_swap(): return lax.ppermute(value, 'row', [(i, i ^ mask) for i in range(16)])  6.81 us
  transfers between devices with their start and end apart: 9, of which 4 were waited for; matrix products, arithmetic and copies ran while one was open for 1% of the time, Pallas kernels for 14%

profile of v4, /device:TPU:1, one launch (start us, length us, event | category | flops | bytes accessed | tf_op | source)
XLA Modules:
  0.0 149.9 jit_solution(15955153729368790590)
XLA Ops:
  0.7 5.2 %shard_map.77 = (f32[8,256,128]{2,1,0:T(8,128)}, bf16[512,1024]{1,0:T(8,128)(2,1)}) custom-call(s32[1]{0:T(128)} %bitcast.1.which_ref, f32[1024,128]{1,0:T(8,128)} %v1_ref.5, f32[1024,128]{1,0:T(8,128)} %v2_ref.7, f32[1024,2048]{1,0:T(8,128)} %base_ref.1), custom_call_target="tpu_custom_call" | custom-call | flops 1610612736 | bytes 6291456 | tf_op jit(solution)/shard_map/pallas_call | solution.py:90
  5.8 1.4 collective-permute-start
  7.3 1.2 copy-done.11
  8.5 1.2 shard_map.79
  9.8 0.8 constant_dynamic-slice_fusion.1
  10.7 0.7 collective-permute-start.2
  11.4 4.7 %shard_map.78.kept_ref = f32[8,256,128]{2,1,0:T(8,128)} custom-call(s32[1]{0:T(128)} %bitcast.which_ref.core_ref, bf16[512,1024]{1,0:T(8,128)(2,1)} %get-tuple-element.18.both_ref, f32[1024,2048]{1,0:T(8,128)} %base_ref.1), custom_call_target="tpu_custom_call" | custom-call | flops 1610612736 | bytes 6291456 | tf_op jit(solution)/shard_map/pallas_call | solution.py:90
  16.1 1.2 copy-done.7
  17.5 32.1 %all_to_all.20.parts_ref = f32[8,336,128]{2,1,0:T(8,128)S(1)} all-to-all(f32[8,336,128]{2,1,0:T(8,128)S(1)} %shard_map.80), channel_id=1, replica_groups={{0,16,32,48,64,80,96,112},{8,24,40,56,72,88,104,120},{1,17,33,49,65,81,..., dimensions={0} | all-to-all | bytes 2752512 | tf_op jit(solution)/shard_map/all_to_all | solution.py:48
  49.5 0.3 shard_map.81
  49.8 1.5 %copy-done.8 = f32[8,656,128]{2,1,0:T(8,128)} copy-done((f32[8,656,128]{2,1,0:T(8,128)}, f32[8,656,128]{2,1,0:T(8,128)S(1)}, u32[]{:S(2)}) %copy-start.8) | copy-done | bytes 2687000
  51.3 3.6 %all-to-all-start.1 = ((f32[8,656,128]{2,1,0:T(8,128)}), f32[8,656,128]{2,1,0:T(8,128)S(1)}, u32[]{:S(2)}, u32[]{:S(2)}) async-start(f32[8,656,128]{2,1,0:T(8,128)} %copy-done.8), calls=%async_computation.1 | async-start | bytes 5373952 | tf_op jit(solution)/shard_map/all_to_all | solution.py:48
  55.0 0.7 collective-permute-start.3
  55.7 35.6 %all-to-all-done.1.mine_ref.parts_ref = f32[8,656,128]{2,1,0:T(8,128)S(1)} async-done(((f32[8,656,128]{2,1,0:T(8,128)}), f32[8,656,128]{2,1,0:T(8,128)S(1)}, u32[]{:S(2)}, u32[]{:S(2)}) %all-to-all-start.1) | async-done | bytes 2687008 | tf_op jit(solution)/shard_map/all_to_all | solution.py:48
  91.3 4.0 %collective-permute-start.4 = (f32[8,656,128]{2,1,0:T(8,128)S(1)}, f32[8,656,128]{2,1,0:T(8,128)}, u32[]{:S(2)}, u32[]{:S(2)}) collective-permute-start(f32[8,656,128]{2,1,0:T(8,128)S(1)} %all-to-all-done.1.mine_ref.parts_ref), channel_id=1, source_target_pairs={{0,8},{8,0},{16,24},{24,16},{32,40},{40,32},{48,56},{56,48},{64,72... | collective-permute-start | bytes 8060936 | tf_op jit(solution)/shard_map/ppermute | solution.py:40
  95.4 1.0 copy-done.2
  96.5 5.5 %all-to-all-start.2 = ((f32[8,160,256]{2,1,0:T(8,128)}), f32[8,160,256]{2,1,0:T(8,128)}, u32[]{:S(2)}, u32[]{:S(2)}) async-start(f32[8,160,256]{2,1,0:T(8,128)} %copy-done.2), calls=%async_computation.2 | async-start | bytes 2621440 | tf_op jit(solution)/shard_map/all_to_all | solution.py:48
  102.0 0.3 fusion
  102.3 0.3 convolution_negate_fusion
  102.6 0.7 select_maximum_fusion.factor_ref
  103.4 10.9 %shard_map.82 = (f32[1024,2048]{1,0:T(8,128)}, f32[1024,256]{1,0:T(8,128)}) custom-call(s32[1]{0:T(128)} %bitcast.which_ref.core_ref, f32[1024,128]{1,0:T(8,128)} %v1_ref.5, f32[1024,128]{1,0:T(8,128)} %v2_ref.7, f32[256,256]{1,0:T(8,128)} %select_maximum_fusion.factor_ref, f32[8,656,128]{2,1,0:T(8,128)} %copy-done, ...), custom_call_target="tpu_custom_call" | custom-call | flops 3221225472 | bytes 16777216 | tf_op jit(solution)/shard_map/pallas_call | solution.py:263
  114.3 8.0 %all-to-all-done.2.p_ref = f32[8,160,256]{2,1,0:T(8,128)} async-done(((f32[8,160,256]{2,1,0:T(8,128)}), f32[8,160,256]{2,1,0:T(8,128)}, u32[]{:S(2)}, u32[]{:S(2)}) %all-to-all-start.2) | async-done | bytes 1310752 | tf_op jit(solution)/shard_map/all_to_all | solution.py:48
  122.4 1.0 slice_reduce_fusion
  123.3 1.3 collective-permute-start.5
  124.6 0.9 collective-permute-done.5
  125.5 0.7 broadcast_in_dim.8
  126.2 4.0 %all-to-all-start.3 = ((f32[8,32,256]{2,1,0:T(8,128)}), f32[8,32,256]{2,1,0:T(8,128)}, u32[]{:S(2)}, u32[]{:S(2)}) async-start(f32[8,32,256]{2,1,0:T(8,128)} %broadcast_in_dim.8), calls=%async_computation.3 | async-start | bytes 524288 | tf_op jit(solution)/shard_map/all_to_all | solution.py:48
  130.3 1.0 copy-done.5
  131.3 1.6 %copy-done.10 = f32[1024,512]{1,0:T(8,128)S(1)} copy-done((f32[1024,512]{1,0:T(8,128)S(1)}, f32[1024,512]{1,0:T(8,128)}, u32[]{:S(2)}) %copy-start.10) | copy-done | bytes 2097176
  132.9 4.6 %shard_map.84 = f32[1024,512]{1,0:T(8,128)} custom-call(s32[1]{0:T(128)} %bitcast.which_ref.core_ref, f32[1024,128]{1,0:T(8,128)S(1)} %copy-done.3, f32[1024,128]{1,0:T(8,128)S(1)} %copy-done.5, f32[256,256]{1,0:T(8,128)S(1)} %copy-done.6, f32[8,656,128]{2,1,0:T(8,128)S(1)} %copy-done.1, f32[8,656,128]{2,1,0:T(8,128)} %collective-permute-done.4.theirs_ref, ...), custom_call_target="tpu_custom_call" | custom-call | flops 1006632960 | bytes 8388608 | tf_op jit(solution)/shard_map/pallas_call | solution.py:353
  137.5 0.9 all-to-all-done.3.gram_ref
  138.4 11.5 %shard_map.85 = f32[1024,2048]{1,0:T(8,128)} custom-call(s32[1]{0:T(128)} %bitcast.which_ref.core_ref, f32[1024,256]{1,0:T(8,128)} %get-tuple-element.27.y_ref, f32[8,160,256]{2,1,0:T(8,128)} %all-to-all-done.2.p_ref, f32[8,32,256]{2,1,0:T(8,128)} %all-to-all-done.3.gram_ref, f32[256,256]{1,0:T(8,128)} %select_maximum_fusion.factor_ref, ...), custom_call_target="tpu_custom_call" | custom-call | flops 3221225472 | bytes 16777216 | tf_op jit(solution)/shard_map/pallas_call | solution.py:305
  (34 shorter events, 0.4 us)
Async XLA Ops:
  0.6 6.6 %copy-start.4 = (f32[1024,128]{1,0:T(8,128)S(1)}, f32[1024,128]{1,0:T(8,128)}, u32[]{:S(2)}) copy-start(f32[1024,128]{1,0:T(8,128)} %v2_ref.7) | copy-start | bytes 1572868
  0.7 6.6 %copy-start.9 = (f32[1024,512]{1,0:T(8,128)S(1)}, f32[1024,512]{1,0:T(8,128)}, u32[]{:S(2)}) copy-start(f32[1024,512]{1,0:T(8,128)} %vectors_ref.3) | copy-start | bytes 6291460
  5.8 10.2 %collective-permute-start = (f32[8,256,128]{2,1,0:T(8,128)}, f32[8,256,128]{2,1,0:T(8,128)S(1)}, u32[]{:S(2)}, u32[]{:S(2)}) collective-permute-start(f32[8,256,128]{2,1,0:T(8,128)} %get-tuple-element.19), channel_id=1, source_target_pairs={{0,8},{8,0},{16,24},{24,16},{32,40},{40,32},{48,56},{56,48},{64,72... | collective-permute-start | bytes 3145736 | tf_op jit(solution)/shard_map/ppermute | solution.py:40
  7.3 1.2 copy-start.11
  9.7 6.4 %collective-permute-start.1 = (f32[8,80,128]{2,1,0:T(8,128)S(1)}, f32[8,80,128]{2,1,0:T(8,128)S(1)}, u32[]{:S(2)}, u32[]{:S(2)}) collective-permute-start(f32[8,80,128]{2,1,0:T(8,128)S(1)} %get-tuple-element.21), channel_id=1, source_target_pairs={{0,8},{8,0},{16,24},{24,16},{32,40},{40,32},{48,56},{56,48},{64,72... | collective-permute-start | bytes 983048 | tf_op jit(solution)/shard_map/ppermute | solution.py:40
  10.7 6.8 %collective-permute-start.2 = (f32[128,256]{1,0:T(8,128)S(1)}, f32[128,256]{1,0:T(8,128)S(1)}, u32[]{:S(2)}, u32[]{:S(2)}) collective-permute-start(f32[128,256]{1,0:T(8,128)S(1)} %pad_maximum_fusion), channel_id=1, source_target_pairs={{0,0},{1,16},{2,32},{3,48},{4,64},{5,80},{6,96},{7,112},{8,8},{9,2... | collective-permute-start | bytes 393224 | tf_op jit(solution)/shard_map/ppermute | solution.py:375
  16.1 1.2 copy-start.7
  49.8 1.5 %copy-start.8 = (f32[8,656,128]{2,1,0:T(8,128)}, f32[8,656,128]{2,1,0:T(8,128)S(1)}, u32[]{:S(2)}) copy-start(f32[8,656,128]{2,1,0:T(8,128)S(1)} %get-tuple-element.24) | copy-start | bytes 8060932
  51.3 40.0 %all-to-all-start.1 = ((f32[8,656,128]{2,1,0:T(8,128)}), f32[8,656,128]{2,1,0:T(8,128)S(1)}, u32[]{:S(2)}, u32[]{:S(2)}) async-start(f32[8,656,128]{2,1,0:T(8,128)} %copy-done.8), calls=%async_computation.1 | async-start | bytes 5373952 | tf_op jit(solution)/shard_map/all_to_all | solution.py:48
  55.0 0.7 collective-permute-start.3
  91.3 10.7 %copy-start = (f32[8,656,128]{2,1,0:T(8,128)}, f32[8,656,128]{2,1,0:T(8,128)S(1)}, u32[]{:S(2)}) copy-start(f32[8,656,128]{2,1,0:T(8,128)S(1)} %all-to-all-done.1.mine_ref.parts_ref) | copy-start | bytes 8060932
  91.3 12.1 %collective-permute-start.4 = (f32[8,656,128]{2,1,0:T(8,128)S(1)}, f32[8,656,128]{2,1,0:T(8,128)}, u32[]{:S(2)}, u32[]{:S(2)}) collective-permute-start(f32[8,656,128]{2,1,0:T(8,128)S(1)} %all-to-all-done.1.mine_ref.parts_ref), channel_id=1, source_target_pairs={{0,8},{8,0},{16,24},{24,16},{32,40},{40,32},{48,56},{56,48},{64,72... | collective-permute-start | bytes 8060936 | tf_op jit(solution)/shard_map/ppermute | solution.py:40
  95.4 1.1 copy-start.2
  96.5 5.6 %copy-start.13 = (f32[128,128]{1,0:T(8,128)S(1)}, f32[128,128]{1,0:T(8,128)}, u32[]{:S(2)}) copy-start(f32[128,128]{1,0:T(8,128)} %param.8) | copy-start | bytes 196612
  96.5 5.9 %copy-start.12 = (f32[128,128]{1,0:T(8,128)S(1)}, f32[128,128]{1,0:T(8,128)}, u32[]{:S(2)}) copy-start(f32[128,128]{1,0:T(8,128)} %param.10) | copy-start | bytes 196612
  96.5 25.9 %all-to-all-start.2 = ((f32[8,160,256]{2,1,0:T(8,128)}), f32[8,160,256]{2,1,0:T(8,128)}, u32[]{:S(2)}, u32[]{:S(2)}) async-start(f32[8,160,256]{2,1,0:T(8,128)} %copy-done.2), calls=%async_computation.2 | async-start | bytes 2621440 | tf_op jit(solution)/shard_map/all_to_all | solution.py:48
  103.4 26.9 %copy-start.3 = (f32[1024,128]{1,0:T(8,128)S(1)}, f32[1024,128]{1,0:T(8,128)}, u32[]{:S(2)}) copy-start(f32[1024,128]{1,0:T(8,128)} %v1_ref.5) | copy-start | bytes 1572868
  103.4 26.9 %copy-start.6 = (f32[256,256]{1,0:T(8,128)S(1)}, f32[256,256]{1,0:T(8,128)}, u32[]{:S(2)}) copy-start(f32[256,256]{1,0:T(8,128)} %select_maximum_fusion.factor_ref) | copy-start | bytes 786436
  103.4 26.9 %copy-start.1 = (f32[8,656,128]{2,1,0:T(8,128)S(1)}, f32[8,656,128]{2,1,0:T(8,128)}, u32[]{:S(2)}) copy-start(f32[8,656,128]{2,1,0:T(8,128)} %copy-done) | copy-start | bytes 8060932
  123.3 2.1 %collective-permute-start.5 = (f32[32,256]{1,0:T(8,128)S(1)}, f32[32,256]{1,0:T(8,128)S(1)}, u32[]{:S(2)}, u32[]{:S(2)}) collective-permute-start(f32[32,256]{1,0:T(8,128)S(1)} %slice_reduce_fusion), channel_id=1, source_target_pairs={{0,8},{8,0},{16,24},{24,16},{32,40},{40,32},{48,56},{56,48},{64,72... | collective-permute-start | bytes 98312 | tf_op jit(solution)/shard_map/ppermute | solution.py:40
  126.2 12.2 %all-to-all-start.3 = ((f32[8,32,256]{2,1,0:T(8,128)}), f32[8,32,256]{2,1,0:T(8,128)}, u32[]{:S(2)}, u32[]{:S(2)}) async-start(f32[8,32,256]{2,1,0:T(8,128)} %broadcast_in_dim.8), calls=%async_computation.3 | async-start | bytes 524288 | tf_op jit(solution)/shard_map/all_to_all | solution.py:48
  130.3 1.0 copy-start.5
  131.3 1.6 %copy-start.10 = (f32[1024,512]{1,0:T(8,128)S(1)}, f32[1024,512]{1,0:T(8,128)}, u32[]{:S(2)}) copy-start(f32[1024,512]{1,0:T(8,128)} %vectors_ref.3) | copy-start | bytes 6291460

commit v5 on v4

--- a/solution.py
+++ b/solution.py
@@ -164,46 +164,48 @@
     for j in range(1, 8):
         total = total + parts_ref[j]
     rows_ref[...] = total[:256].T
-    gram = three(total[:256], v_ref[...])
     for j in range(8):
         out_ref[j, :256] = total[:256]
         out_ref[j, 256:384] = v_ref[:, :128]
         out_ref[j, 384:512] = v_ref[:, 128:]
-        out_ref[j, 512:576] = total[256:320]
-        out_ref[j, 576:608] = gram[j * 32 : j * 32 + 32, :128]
-        out_ref[j, 608:640] = gram[j * 32 : j * 32 + 32, 128:]
-        out_ref[j, 640:] = total[320:]
+        out_ref[j, 512:] = total[256:]
 
 
 def chunk_product(parts, v):
     return pl.pallas_call(
         chunk_kernel,
-        out_shape=[jax.ShapeDtypeStruct((8, 656, 128), F32), jax.ShapeDtypeStruct((128, 256), F32)],
+        out_shape=[jax.ShapeDtypeStruct((8, 592, 128), F32), jax.ShapeDtypeStruct((128, 256), F32)],
         compiler_params=params(16),
-        cost_estimate=cost(3 * 2 * 256 * 256 * 128, 2**22),
+        cost_estimate=cost(2**20, 2**22),
     )(parts, v)
 
 
-def rows_kernel(parts_ref, rows_ref, out_ref):
-    total = parts_ref[0]
-    for j in range(1, 8):
-        total = total + parts_ref[j]
+def rows_kernel(chip_ref, p_ref, v_ref, rows_ref, out_ref):
+    total = jnp.zeros((32, 256), F32)
+    for j in range(8):
+        total = total + three(p_ref[j], jnp.concatenate([v_ref[j, :128], v_ref[j, 128:]], axis=1))
     for j in range(8):
         out_ref[j, :128] = rows_ref[...]
-        out_ref[j, 128:, :128] = total[:32]
-        out_ref[j, 128:, 128:] = total[32:]
-
-
-def rows_pack(parts, rows):
+        out_ref[j, 128:] = total
+
+
+def rows_pack(chip, parts, rows):
     return pl.pallas_call(
         rows_kernel,
-        grid=(1,),
-        in_specs=[pl.BlockSpec((8, 64, 128), lambda i: (0, 9, 0)), pl.BlockSpec((128, 256), lambda i: (0, 0))],
-        out_specs=pl.BlockSpec((8, 160, 256), lambda i: (0, 0, 0)),
+        grid_spec=pltpu.PrefetchScalarGridSpec(
+            num_scalar_prefetch=1,
+            grid=(1,),
+            in_specs=[
+                pl.BlockSpec((8, 32, 128), lambda i, chip: (0, chip[0], 0)),
+                pl.BlockSpec((8, 256, 128), lambda i, chip: (0, 1, 0)),
+                pl.BlockSpec((128, 256), lambda i, chip: (0, 0)),
+            ],
+            out_specs=pl.BlockSpec((8, 160, 256), lambda i, chip: (0, 0, 0)),
+        ),
         out_shape=jax.ShapeDtypeStruct((8, 160, 256), F32),
         compiler_params=params(16),
-        cost_estimate=cost(2**20, 2**22),
-    )(parts, rows)
+        cost_estimate=cost(3 * 2 * 32 * 1024 * 256, 2**22),
+    )(chip, parts, parts, rows)
 
 
 def turned_three(left, right):
@@ -367,6 +369,7 @@
 
 def shards(matrix, v1, f1, v2, f2, vectors):
     core = lax.axis_index("row") % 2
+    chip = lax.axis_index("row") // 2
     col = lax.axis_index("col")
 
     v_chunk = jnp.concatenate(
@@ -389,10 +392,10 @@
     over = lax.ppermute(over, BOTH, turn_map())
     got, over = lax.optimization_barrier((got, over))
 
-    p_rows = exchange(rows_pack(got, over), "col", None)
+    p_rows = exchange(rows_pack(chip[None], got, over), "col", None)
 
     theirs = row_swap(got, 1)
-    cross = got[:, 640:].reshape(128, 128)
+    cross = got[:, 576:].reshape(128, 128)
     a_right = -small(small(f1, cross), f2)
     factor = jnp.concatenate(
         [jnp.concatenate([f1, a_right], axis=1), jnp.concatenate([jnp.zeros_like(f2), f2], axis=1)], axis=0

time: 151 us -> 147 us (0.974)
  waiting for transfers between devices: 45.4 us -> 41.3 us
    all_to_all x3, waiting for transfers between devices: 44.5 us -> 40.4 us  [exchange(): lax.all_to_all(value, axis, 0, 0, axis_index_groups=groups, tiled=True)]
  transfers between devices with their start and end apart: 9 -> 9, of which waited for: 4 -> 4; matrix products, arithmetic and copies ran while one was open for 1% -> 1% of each run, Pallas kernels for 14% -> 15%
where the time goes in v5:
time: 147 us; the launch traced here: 146 us
  waiting for transfers between devices  41.3 us (28%)
  Pallas kernels  38.9 us (26%)
  blocking collectives  32.1 us (22%)
  starting transfers between devices  21.5 us (15%)
  local copies, waits for them, and re-layouts  9.07 us (6%)
  other arithmetic  1.71 us (1%)
    all_to_all x3, waiting for transfers between devices, exchange(): lax.all_to_all(value, axis, 0, 0, axis_index_groups=groups, tiled=True)  40.4 us
    all_to_all x1, blocking collectives, exchange(): lax.all_to_all(value, axis, 0, 0, axis_index_groups=groups, tiled=True)  32.1 us
    all_to_all x3, starting transfers between devices, exchange(): lax.all_to_all(value, axis, 0, 0, axis_index_groups=groups, tiled=True)  13.2 us
    pallas_call x1, Pallas kernels, last_product(): pl.pallas_call(last_kernel, grid_spec=pltpu.PrefetchScalarGridSpec(num_sc...  11.5 us
    pallas_call x1, Pallas kernels, first_product(): pl.pallas_call(first_kernel, grid_spec=pltpu.PrefetchScalarGridSpec(num_s...  11 us
    pallas_call x2, Pallas kernels, half_product(): pl.pallas_call(kernel, grid_spec=pltpu.PrefetchScalarGridSpec(num_scalar_...  9.86 us
    unnamed x28, local copies, waits for them, and re-layouts  7.48 us
    ppermute x4, starting transfers between devices, row_swap(): return lax.ppermute(value, 'row', [(i, i ^ mask) for i in range(16)])  7.04 us
  transfers between devices with their start and end apart: 9, of which 4 were waited for; matrix products, arithmetic and copies ran while one was open for 1% of the time, Pallas kernels for 15%

profile of v5, /device:TPU:1, one launch (start us, length us, event | category | flops | bytes accessed | tf_op | source)
XLA Modules:
  0.0 145.9 jit_solution(1064387733598486443)
XLA Ops:
  0.7 5.2 %shard_map.77 = (f32[8,256,128]{2,1,0:T(8,128)}, bf16[512,1024]{1,0:T(8,128)(2,1)}) custom-call(s32[1]{0:T(128)} %bitcast.1.which_ref, f32[1024,128]{1,0:T(8,128)} %v1_ref.5, f32[1024,128]{1,0:T(8,128)} %v2_ref.7, f32[1024,2048]{1,0:T(8,128)} %base_ref.1), custom_call_target="tpu_custom_call" | custom-call | flops 1610612736 | bytes 6291456 | tf_op jit(solution)/shard_map/pallas_call | solution.py:90
  5.8 1.4 collective-permute-start
  7.3 1.2 copy-done.11
  8.5 1.2 shard_map.79
  9.8 0.8 constant_dynamic-slice_fusion.1
  10.7 0.7 collective-permute-start.2
  11.4 4.7 %shard_map.78.kept_ref = f32[8,256,128]{2,1,0:T(8,128)} custom-call(s32[1]{0:T(128)} %bitcast.which_ref.core_ref, bf16[512,1024]{1,0:T(8,128)(2,1)} %get-tuple-element.18.both_ref, f32[1024,2048]{1,0:T(8,128)} %base_ref.1), custom_call_target="tpu_custom_call" | custom-call | flops 1610612736 | bytes 6291456 | tf_op jit(solution)/shard_map/pallas_call | solution.py:90
  16.1 1.2 copy-done.7
  17.4 32.1 %all_to_all.20.parts_ref = f32[8,336,128]{2,1,0:T(8,128)S(1)} all-to-all(f32[8,336,128]{2,1,0:T(8,128)S(1)} %shard_map.80), channel_id=1, replica_groups={{0,16,32,48,64,80,96,112},{8,24,40,56,72,88,104,120},{1,17,33,49,65,81,..., dimensions={0} | all-to-all | bytes 2752512 | tf_op jit(solution)/shard_map/all_to_all | solution.py:48
  49.7 1.4 copy-done.8
  51.1 3.6 %all-to-all-start.1 = ((f32[8,592,128]{2,1,0:T(8,128)}), f32[8,592,128]{2,1,0:T(8,128)S(1)}, u32[]{:S(2)}, u32[]{:S(2)}) async-start(f32[8,592,128]{2,1,0:T(8,128)} %copy-done.8), calls=%async_computation.1 | async-start | bytes 4849664 | tf_op jit(solution)/shard_map/all_to_all | solution.py:48
  54.8 0.7 collective-permute-start.3
  55.4 31.9 %all-to-all-done.1.mine_ref.p_ref.v_ref = f32[8,592,128]{2,1,0:T(8,128)S(1)} async-done(((f32[8,592,128]{2,1,0:T(8,128)}), f32[8,592,128]{2,1,0:T(8,128)S(1)}, u32[]{:S(2)}, u32[]{:S(2)}) %all-to-all-start.1) | async-done | bytes 2424864 | tf_op jit(solution)/shard_map/all_to_all | solution.py:48
  87.3 4.0 %collective-permute-start.4 = (f32[8,592,128]{2,1,0:T(8,128)S(1)}, f32[8,592,128]{2,1,0:T(8,128)}, u32[]{:S(2)}, u32[]{:S(2)}) collective-permute-start(f32[8,592,128]{2,1,0:T(8,128)S(1)} %all-to-all-done.1.mine_ref.p_ref.v_ref), channel_id=1, source_target_pairs={{0,8},{8,0},{16,24},{24,16},{32,40},{40,32},{48,56},{56,48},{64,72... | collective-permute-start | bytes 7274504 | tf_op jit(solution)/shard_map/ppermute | solution.py:40
  91.4 0.4 shard_map.83
  91.7 1.0 copy-done.2
  92.8 5.5 %all-to-all-start.2 = ((f32[8,160,256]{2,1,0:T(8,128)}), f32[8,160,256]{2,1,0:T(8,128)}, u32[]{:S(2)}, u32[]{:S(2)}) async-start(f32[8,160,256]{2,1,0:T(8,128)} %copy-done.2), calls=%async_computation.2 | async-start | bytes 2621440 | tf_op jit(solution)/shard_map/all_to_all | solution.py:48
  98.3 0.3 fusion
  98.6 0.3 convolution_negate_fusion
  98.9 0.7 select_maximum_fusion.factor_ref
  99.7 11.0 %shard_map.82 = (f32[1024,2048]{1,0:T(8,128)}, f32[1024,256]{1,0:T(8,128)}) custom-call(s32[1]{0:T(128)} %bitcast.which_ref.core_ref, f32[1024,128]{1,0:T(8,128)} %v1_ref.5, f32[1024,128]{1,0:T(8,128)} %v2_ref.7, f32[256,256]{1,0:T(8,128)} %select_maximum_fusion.factor_ref, f32[8,592,128]{2,1,0:T(8,128)} %copy-done, ...), custom_call_target="tpu_custom_call" | custom-call | flops 3221225472 | bytes 16777216 | tf_op jit(solution)/shard_map/pallas_call | solution.py:265
  110.6 7.6 %all-to-all-done.2.p_ref = f32[8,160,256]{2,1,0:T(8,128)} async-done(((f32[8,160,256]{2,1,0:T(8,128)}), f32[8,160,256]{2,1,0:T(8,128)}, u32[]{:S(2)}, u32[]{:S(2)}) %all-to-all-start.2) | async-done | bytes 1310752 | tf_op jit(solution)/shard_map/all_to_all | solution.py:48
  118.2 1.0 slice_reduce_fusion
  119.2 1.5 %collective-permute-start.5 = (f32[32,256]{1,0:T(8,128)S(1)}, f32[32,256]{1,0:T(8,128)S(1)}, u32[]{:S(2)}, u32[]{:S(2)}) collective-permute-start(f32[32,256]{1,0:T(8,128)S(1)} %slice_reduce_fusion), channel_id=1, source_target_pairs={{0,8},{8,0},{16,24},{24,16},{32,40},{40,32},{48,56},{56,48},{64,72... | collective-permute-start | bytes 98312 | tf_op jit(solution)/shard_map/ppermute | solution.py:40
  120.7 0.9 collective-permute-done.5
  121.5 0.7 broadcast_in_dim.11
  122.3 4.0 %all-to-all-start.3 = ((f32[8,32,256]{2,1,0:T(8,128)}), f32[8,32,256]{2,1,0:T(8,128)}, u32[]{:S(2)}, u32[]{:S(2)}) async-start(f32[8,32,256]{2,1,0:T(8,128)} %broadcast_in_dim.11), calls=%async_computation.3 | async-start | bytes 524288 | tf_op jit(solution)/shard_map/all_to_all | solution.py:48
  126.3 0.9 copy-done.6
  127.3 1.6 %copy-done.10 = f32[1024,512]{1,0:T(8,128)S(1)} copy-done((f32[1024,512]{1,0:T(8,128)S(1)}, f32[1024,512]{1,0:T(8,128)}, u32[]{:S(2)}) %copy-start.10) | copy-done | bytes 2097176
  128.9 4.6 %shard_map.84 = f32[1024,512]{1,0:T(8,128)} custom-call(s32[1]{0:T(128)} %bitcast.which_ref.core_ref, f32[1024,128]{1,0:T(8,128)S(1)} %copy-done.3, f32[1024,128]{1,0:T(8,128)S(1)} %copy-done.5, f32[256,256]{1,0:T(8,128)S(1)} %copy-done.6, f32[8,592,128]{2,1,0:T(8,128)S(1)} %copy-done.1, f32[8,592,128]{2,1,0:T(8,128)} %collective-permute-done.4.theirs_ref, ...), custom_call_target="tpu_custom_call" | custom-call | flops 1006632960 | bytes 8388608 | tf_op jit(solution)/shard_map/pallas_call | solution.py:355
  133.5 0.9 all-to-all-done.3.gram_ref
  134.4 11.5 %shard_map.85 = f32[1024,2048]{1,0:T(8,128)} custom-call(s32[1]{0:T(128)} %bitcast.which_ref.core_ref, f32[1024,256]{1,0:T(8,128)} %get-tuple-element.27.y_ref, f32[8,160,256]{2,1,0:T(8,128)} %all-to-all-done.2.p_ref, f32[8,32,256]{2,1,0:T(8,128)} %all-to-all-done.3.gram_ref, f32[256,256]{1,0:T(8,128)} %select_maximum_fusion.factor_ref, ...), custom_call_target="tpu_custom_call" | custom-call | flops 3221225472 | bytes 16777216 | tf_op jit(solution)/shard_map/pallas_call | solution.py:307
  (34 shorter events, 0.5 us)
Async XLA Ops:
  0.6 6.6 %copy-start.4 = (f32[1024,128]{1,0:T(8,128)S(1)}, f32[1024,128]{1,0:T(8,128)}, u32[]{:S(2)}) copy-start(f32[1024,128]{1,0:T(8,128)} %v2_ref.7) | copy-start | bytes 1572868
  0.7 6.6 %copy-start.9 = (f32[1024,512]{1,0:T(8,128)S(1)}, f32[1024,512]{1,0:T(8,128)}, u32[]{:S(2)}) copy-start(f32[1024,512]{1,0:T(8,128)} %vectors_ref.3) | copy-start | bytes 6291460
  5.8 10.2 %collective-permute-start = (f32[8,256,128]{2,1,0:T(8,128)}, f32[8,256,128]{2,1,0:T(8,128)S(1)}, u32[]{:S(2)}, u32[]{:S(2)}) collective-permute-start(f32[8,256,128]{2,1,0:T(8,128)} %get-tuple-element.19), channel_id=1, source_target_pairs={{0,8},{8,0},{16,24},{24,16},{32,40},{40,32},{48,56},{56,48},{64,72... | collective-permute-start | bytes 3145736 | tf_op jit(solution)/shard_map/ppermute | solution.py:40
  7.3 1.2 copy-start.11
  9.7 6.3 %collective-permute-start.1 = (f32[8,80,128]{2,1,0:T(8,128)S(1)}, f32[8,80,128]{2,1,0:T(8,128)S(1)}, u32[]{:S(2)}, u32[]{:S(2)}) collective-permute-start(f32[8,80,128]{2,1,0:T(8,128)S(1)} %get-tuple-element.21), channel_id=1, source_target_pairs={{0,8},{8,0},{16,24},{24,16},{32,40},{40,32},{48,56},{56,48},{64,72... | collective-permute-start | bytes 983048 | tf_op jit(solution)/shard_map/ppermute | solution.py:40
  10.7 6.8 %collective-permute-start.2 = (f32[128,256]{1,0:T(8,128)S(1)}, f32[128,256]{1,0:T(8,128)S(1)}, u32[]{:S(2)}, u32[]{:S(2)}) collective-permute-start(f32[128,256]{1,0:T(8,128)S(1)} %pad_maximum_fusion), channel_id=1, source_target_pairs={{0,0},{1,16},{2,32},{3,48},{4,64},{5,80},{6,96},{7,112},{8,8},{9,2... | collective-permute-start | bytes 393224 | tf_op jit(solution)/shard_map/ppermute | solution.py:378
  16.1 1.2 copy-start.7
  49.7 1.4 copy-start.8
  51.1 36.2 %all-to-all-start.1 = ((f32[8,592,128]{2,1,0:T(8,128)}), f32[8,592,128]{2,1,0:T(8,128)S(1)}, u32[]{:S(2)}, u32[]{:S(2)}) async-start(f32[8,592,128]{2,1,0:T(8,128)} %copy-done.8), calls=%async_computation.1 | async-start | bytes 4849664 | tf_op jit(solution)/shard_map/all_to_all | solution.py:48
  54.8 0.7 collective-permute-start.3
  87.3 11.0 %copy-start = (f32[8,592,128]{2,1,0:T(8,128)}, f32[8,592,128]{2,1,0:T(8,128)S(1)}, u32[]{:S(2)}) copy-start(f32[8,592,128]{2,1,0:T(8,128)S(1)} %all-to-all-done.1.mine_ref.p_ref.v_ref) | copy-start | bytes 7274500
  87.3 12.3 %collective-permute-start.4 = (f32[8,592,128]{2,1,0:T(8,128)S(1)}, f32[8,592,128]{2,1,0:T(8,128)}, u32[]{:S(2)}, u32[]{:S(2)}) collective-permute-start(f32[8,592,128]{2,1,0:T(8,128)S(1)} %all-to-all-done.1.mine_ref.p_ref.v_ref), channel_id=1, source_target_pairs={{0,8},{8,0},{16,24},{24,16},{32,40},{40,32},{48,56},{56,48},{64,72... | collective-permute-start | bytes 7274504 | tf_op jit(solution)/shard_map/ppermute | solution.py:40
  91.7 1.1 copy-start.2
  92.8 5.5 %copy-start.13 = (f32[128,128]{1,0:T(8,128)S(1)}, f32[128,128]{1,0:T(8,128)}, u32[]{:S(2)}) copy-start(f32[128,128]{1,0:T(8,128)} %param.8) | copy-start | bytes 196612
  92.8 5.8 %copy-start.12 = (f32[128,128]{1,0:T(8,128)S(1)}, f32[128,128]{1,0:T(8,128)}, u32[]{:S(2)}) copy-start(f32[128,128]{1,0:T(8,128)} %param.10) | copy-start | bytes 196612
  92.8 25.4 %all-to-all-start.2 = ((f32[8,160,256]{2,1,0:T(8,128)}), f32[8,160,256]{2,1,0:T(8,128)}, u32[]{:S(2)}, u32[]{:S(2)}) async-start(f32[8,160,256]{2,1,0:T(8,128)} %copy-done.2), calls=%async_computation.2 | async-start | bytes 2621440 | tf_op jit(solution)/shard_map/all_to_all | solution.py:48
  99.6 26.7 %copy-start.3 = (f32[1024,128]{1,0:T(8,128)S(1)}, f32[1024,128]{1,0:T(8,128)}, u32[]{:S(2)}) copy-start(f32[1024,128]{1,0:T(8,128)} %v1_ref.5) | copy-start | bytes 1572868
  99.7 26.7 %copy-start.5 = (f32[1024,128]{1,0:T(8,128)S(1)}, f32[1024,128]{1,0:T(8,128)}, u32[]{:S(2)}) copy-start(f32[1024,128]{1,0:T(8,128)} %v2_ref.7) | copy-start | bytes 1572868
  99.7 26.7 %copy-start.1 = (f32[8,592,128]{2,1,0:T(8,128)S(1)}, f32[8,592,128]{2,1,0:T(8,128)}, u32[]{:S(2)}) copy-start(f32[8,592,128]{2,1,0:T(8,128)} %copy-done) | copy-start | bytes 7274500
  119.2 2.4 %collective-permute-start.5 = (f32[32,256]{1,0:T(8,128)S(1)}, f32[32,256]{1,0:T(8,128)S(1)}, u32[]{:S(2)}, u32[]{:S(2)}) collective-permute-start(f32[32,256]{1,0:T(8,128)S(1)} %slice_reduce_fusion), channel_id=1, source_target_pairs={{0,8},{8,0},{16,24},{24,16},{32,40},{40,32},{48,56},{56,48},{64,72... | collective-permute-start | bytes 98312 | tf_op jit(solution)/shard_map/ppermute | solution.py:40
  122.3 12.2 %all-to-all-start.3 = ((f32[8,32,256]{2,1,0:T(8,128)}), f32[8,32,256]{2,1,0:T(8,128)}, u32[]{:S(2)}, u32[]{:S(2)}) async-start(f32[8,32,256]{2,1,0:T(8,128)} %broadcast_in_dim.11), calls=%async_computation.3 | async-start | bytes 524288 | tf_op jit(solution)/shard_map/all_to_all | solution.py:48
  126.3 1.0 copy-start.6
  127.3 1.6 %copy-start.10 = (f32[1024,512]{1,0:T(8,128)S(1)}, f32[1024,512]{1,0:T(8,128)}, u32[]{:S(2)}) copy-start(f32[1024,512]{1,0:T(8,128)} %vectors_ref.3) | copy-start | bytes 6291460

commit v6 on v5

--- a/solution.py
+++ b/solution.py
@@ -362,7 +362,7 @@
             scratch_shapes=[pltpu.VMEM((256, 512), F32)],
         ),
         out_shape=jax.ShapeDtypeStruct(vectors.shape, F32),
-        compiler_params=params(24),
+        compiler_params=params(58),
         cost_estimate=cost(3 * 2 * 1280 * 256 * 512, 2**23),
     )(core, v1, v2, factor, mine, theirs, vectors)
 

time: 147 us -> 147 us (level)
  local copies, waits for them, and re-layouts: 9.07 us -> 7.23 us
    unnamed x28 -> x20, local copies, waits for them, and re-layouts: 7.48 us -> 5.65 us
  transfers between devices with their start and end apart: 9 -> 9, of which waited for: 4 -> 4; matrix products, arithmetic and copies ran while one was open for 1% -> 1% of each run, Pallas kernels for 15% -> 16%
where the time goes in v6:
time: 147 us; the launch traced here: 145 us
  waiting for transfers between devices  42.2 us (29%)
  Pallas kernels  39.9 us (27%)
  blocking collectives  32.1 us (22%)
  starting transfers between devices  20.9 us (14%)
  local copies, waits for them, and re-layouts  7.23 us (5%)
  other arithmetic  1.73 us (1%)
    all_to_all x3, waiting for transfers between devices, exchange(): lax.all_to_all(value, axis, 0, 0, axis_index_groups=groups, tiled=True)  41.3 us
    all_to_all x1, blocking collectives, exchange(): lax.all_to_all(value, axis, 0, 0, axis_index_groups=groups, tiled=True)  32.1 us
    all_to_all x3, starting transfers between devices, exchange(): lax.all_to_all(value, axis, 0, 0, axis_index_groups=groups, tiled=True)  12.5 us
    pallas_call x1, Pallas kernels, last_product(): pl.pallas_call(last_kernel, grid_spec=pltpu.PrefetchScalarGridSpec(num_sc...  11.5 us
    pallas_call x1, Pallas kernels, first_product(): pl.pallas_call(first_kernel, grid_spec=pltpu.PrefetchScalarGridSpec(num_s...  10.8 us
    pallas_call x2, Pallas kernels, half_product(): pl.pallas_call(kernel, grid_spec=pltpu.PrefetchScalarGridSpec(num_scalar_...  9.84 us
    ppermute x4, starting transfers between devices, row_swap(): return lax.ppermute(value, 'row', [(i, i ^ mask) for i in range(16)])  7.03 us
    pallas_call x1, Pallas kernels, back_product(): pl.pallas_call(back_kernel, grid_spec=pltpu.PrefetchScalarGridSpec(num_sc...  5.81 us
  transfers between devices with their start and end apart: 9, of which 4 were waited for; matrix products, arithmetic and copies ran while one was open for 1% of the time, Pallas kernels for 16%

profile of v6, /device:TPU:1, one launch (start us, length us, event | category | flops | bytes accessed | tf_op | source)
XLA Modules:
  0.0 145.4 jit_solution(9363248980154379041)
XLA Ops:
  0.7 5.2 %shard_map.77 = (f32[8,256,128]{2,1,0:T(8,128)}, bf16[512,1024]{1,0:T(8,128)(2,1)}) custom-call(s32[1]{0:T(128)} %bitcast.1.which_ref, f32[1024,128]{1,0:T(8,128)} %v1_ref.5, f32[1024,128]{1,0:T(8,128)} %v2_ref.7, f32[1024,2048]{1,0:T(8,128)} %base_ref.1), custom_call_target="tpu_custom_call" | custom-call | flops 1610612736 | bytes 6291456 | tf_op jit(solution)/shard_map/pallas_call | solution.py:90
  5.8 1.4 collective-permute-start
  7.3 1.2 copy-done.6
  8.5 1.2 shard_map.79
  9.8 0.8 constant_dynamic-slice_fusion.1
  10.7 0.7 collective-permute-start.2
  11.4 4.7 %shard_map.78.kept_ref = f32[8,256,128]{2,1,0:T(8,128)} custom-call(s32[1]{0:T(128)} %bitcast.which_ref.core_ref, bf16[512,1024]{1,0:T(8,128)(2,1)} %get-tuple-element.18.both_ref, f32[1024,2048]{1,0:T(8,128)} %base_ref.1), custom_call_target="tpu_custom_call" | custom-call | flops 1610612736 | bytes 6291456 | tf_op jit(solution)/shard_map/pallas_call | solution.py:90
  16.1 1.2 copy-done.3
  17.4 32.1 %all_to_all.20.parts_ref = f32[8,336,128]{2,1,0:T(8,128)S(1)} all-to-all(f32[8,336,128]{2,1,0:T(8,128)S(1)} %shard_map.80), channel_id=1, replica_groups={{0,16,32,48,64,80,96,112},{8,24,40,56,72,88,104,120},{1,17,33,49,65,81,..., dimensions={0} | all-to-all | bytes 2752512 | tf_op jit(solution)/shard_map/all_to_all | solution.py:48
  49.5 0.2 shard_map.81
  49.7 1.4 copy-done.4
  51.1 3.6 %all-to-all-start.1 = ((f32[8,592,128]{2,1,0:T(8,128)}), f32[8,592,128]{2,1,0:T(8,128)S(1)}, u32[]{:S(2)}, u32[]{:S(2)}) async-start(f32[8,592,128]{2,1,0:T(8,128)} %copy-done.4), calls=%async_computation.1 | async-start | bytes 4849664 | tf_op jit(solution)/shard_map/all_to_all | solution.py:48
  54.8 0.7 collective-permute-start.3
  55.4 31.9 %all-to-all-done.1.mine_ref.p_ref.v_ref = f32[8,592,128]{2,1,0:T(8,128)S(1)} async-done(((f32[8,592,128]{2,1,0:T(8,128)}), f32[8,592,128]{2,1,0:T(8,128)S(1)}, u32[]{:S(2)}, u32[]{:S(2)}) %all-to-all-start.1) | async-done | bytes 2424864 | tf_op jit(solution)/shard_map/all_to_all | solution.py:48
  87.3 4.0 %collective-permute-start.4 = (f32[8,592,128]{2,1,0:T(8,128)S(1)}, f32[8,592,128]{2,1,0:T(8,128)}, u32[]{:S(2)}, u32[]{:S(2)}) collective-permute-start(f32[8,592,128]{2,1,0:T(8,128)S(1)} %all-to-all-done.1.mine_ref.p_ref.v_ref), channel_id=1, source_target_pairs={{0,8},{8,0},{16,24},{24,16},{32,40},{40,32},{48,56},{56,48},{64,72... | collective-permute-start | bytes 7274504 | tf_op jit(solution)/shard_map/ppermute | solution.py:40
  91.4 0.4 shard_map.83
  91.7 1.0 copy-done.1
  92.8 5.5 %all-to-all-start.2 = ((f32[8,160,256]{2,1,0:T(8,128)}), f32[8,160,256]{2,1,0:T(8,128)}, u32[]{:S(2)}, u32[]{:S(2)}) async-start(f32[8,160,256]{2,1,0:T(8,128)} %copy-done.1), calls=%async_computation.2 | async-start | bytes 2621440 | tf_op jit(solution)/shard_map/all_to_all | solution.py:48
  98.3 0.3 fusion
  98.6 0.3 convolution_negate_fusion
  98.9 0.7 select_maximum_fusion.factor_ref
  99.7 10.8 %shard_map.82 = (f32[1024,2048]{1,0:T(8,128)}, f32[1024,256]{1,0:T(8,128)}) custom-call(s32[1]{0:T(128)} %bitcast.which_ref.core_ref, f32[1024,128]{1,0:T(8,128)} %v1_ref.5, f32[1024,128]{1,0:T(8,128)} %v2_ref.7, f32[256,256]{1,0:T(8,128)} %select_maximum_fusion.factor_ref, f32[8,592,128]{2,1,0:T(8,128)} %copy-done, ...), custom_call_target="tpu_custom_call" | custom-call | flops 3221225472 | bytes 16777216 | tf_op jit(solution)/shard_map/pallas_call | solution.py:265
  110.5 7.7 %all-to-all-done.2.p_ref = f32[8,160,256]{2,1,0:T(8,128)} async-done(((f32[8,160,256]{2,1,0:T(8,128)}), f32[8,160,256]{2,1,0:T(8,128)}, u32[]{:S(2)}, u32[]{:S(2)}) %all-to-all-start.2) | async-done | bytes 1310752 | tf_op jit(solution)/shard_map/all_to_all | solution.py:48
  118.2 1.0 slice_reduce_fusion
  119.2 1.5 %collective-permute-start.5 = (f32[32,256]{1,0:T(8,128)S(1)}, f32[32,256]{1,0:T(8,128)S(1)}, u32[]{:S(2)}, u32[]{:S(2)}) collective-permute-start(f32[32,256]{1,0:T(8,128)S(1)} %slice_reduce_fusion), channel_id=1, source_target_pairs={{0,8},{8,0},{16,24},{24,16},{32,40},{40,32},{48,56},{56,48},{64,72... | collective-permute-start | bytes 98312 | tf_op jit(solution)/shard_map/ppermute | solution.py:40
  120.7 0.9 collective-permute-done.5
  121.5 0.7 broadcast_in_dim.11
  122.3 3.4 %all-to-all-start.3 = ((f32[8,32,256]{2,1,0:T(8,128)}), f32[8,32,256]{2,1,0:T(8,128)S(1)}, u32[]{:S(2)}, u32[]{:S(2)}) async-start(f32[8,32,256]{2,1,0:T(8,128)} %broadcast_in_dim.11), calls=%async_computation.3 | async-start | bytes 524288 | tf_op jit(solution)/shard_map/all_to_all | solution.py:48
  125.7 5.8 %shard_map.84 = f32[1024,512]{1,0:T(8,128)} custom-call(s32[1]{0:T(128)} %bitcast.which_ref.core_ref, f32[1024,128]{1,0:T(8,128)} %v1_ref.5, f32[1024,128]{1,0:T(8,128)} %v2_ref.7, f32[256,256]{1,0:T(8,128)} %select_maximum_fusion.factor_ref, f32[8,592,128]{2,1,0:T(8,128)} %copy-done, f32[8,592,128]{2,1,0:T(8,128)} %collective-permute-done.4.theirs_ref, ...), custom_call_target="tpu_custom_call" | custom-call | flops 1006632960 | bytes 8388608 | tf_op jit(solution)/shard_map/pallas_call | solution.py:355
  131.5 1.7 %all-to-all-done.3.gram_ref = f32[8,32,256]{2,1,0:T(8,128)S(1)} async-done(((f32[8,32,256]{2,1,0:T(8,128)}), f32[8,32,256]{2,1,0:T(8,128)S(1)}, u32[]{:S(2)}, u32[]{:S(2)}) %all-to-all-start.3) | async-done | bytes 262176 | tf_op jit(solution)/shard_map/all_to_all | solution.py:48
  133.2 0.7 copy-done.7
  133.9 11.5 %shard_map.85 = f32[1024,2048]{1,0:T(8,128)} custom-call(s32[1]{0:T(128)} %bitcast.which_ref.core_ref, f32[1024,256]{1,0:T(8,128)} %get-tuple-element.27.y_ref, f32[8,160,256]{2,1,0:T(8,128)} %all-to-all-done.2.p_ref, f32[8,32,256]{2,1,0:T(8,128)} %copy-done.7, f32[256,256]{1,0:T(8,128)} %select_maximum_fusion.factor_ref, f32[8,592,128]{2,1,0:T(8,128)} %copy-done, ...), custom_call_target="tpu_custom_call" | custom-call | flops 3221225472 | bytes 16777216 | tf_op jit(solution)/shard_map/pallas_call | solution.py:307
  (26 shorter events, 0.3 us)
Async XLA Ops:
  0.6 6.6 %copy-start.2 = (f32[1024,128]{1,0:T(8,128)S(1)}, f32[1024,128]{1,0:T(8,128)}, u32[]{:S(2)}) copy-start(f32[1024,128]{1,0:T(8,128)} %v2_ref.7) | copy-start | bytes 1572868
  0.7 6.6 %copy-start.5 = (f32[1024,512]{1,0:T(8,128)S(1)}, f32[1024,512]{1,0:T(8,128)}, u32[]{:S(2)}) copy-start(f32[1024,512]{1,0:T(8,128)} %vectors_ref.3) | copy-start | bytes 6291460
  5.8 10.2 %collective-permute-start = (f32[8,256,128]{2,1,0:T(8,128)}, f32[8,256,128]{2,1,0:T(8,128)S(1)}, u32[]{:S(2)}, u32[]{:S(2)}) collective-permute-start(f32[8,256,128]{2,1,0:T(8,128)} %get-tuple-element.19), channel_id=1, source_target_pairs={{0,8},{8,0},{16,24},{24,16},{32,40},{40,32},{48,56},{56,48},{64,72... | collective-permute-start | bytes 3145736 | tf_op jit(solution)/shard_map/ppermute | solution.py:40
  7.3 1.2 copy-start.6
  9.7 6.3 %collective-permute-start.1 = (f32[8,80,128]{2,1,0:T(8,128)S(1)}, f32[8,80,128]{2,1,0:T(8,128)S(1)}, u32[]{:S(2)}, u32[]{:S(2)}) collective-permute-start(f32[8,80,128]{2,1,0:T(8,128)S(1)} %get-tuple-element.21), channel_id=1, source_target_pairs={{0,8},{8,0},{16,24},{24,16},{32,40},{40,32},{48,56},{56,48},{64,72... | collective-permute-start | bytes 983048 | tf_op jit(solution)/shard_map/ppermute | solution.py:40
  10.7 6.7 %collective-permute-start.2 = (f32[128,256]{1,0:T(8,128)S(1)}, f32[128,256]{1,0:T(8,128)S(1)}, u32[]{:S(2)}, u32[]{:S(2)}) collective-permute-start(f32[128,256]{1,0:T(8,128)S(1)} %pad_maximum_fusion), channel_id=1, source_target_pairs={{0,0},{1,16},{2,32},{3,48},{4,64},{5,80},{6,96},{7,112},{8,8},{9,2... | collective-permute-start | bytes 393224 | tf_op jit(solution)/shard_map/ppermute | solution.py:378
  16.1 1.2 copy-start.3
  49.7 1.4 copy-start.4
  51.1 36.2 %all-to-all-start.1 = ((f32[8,592,128]{2,1,0:T(8,128)}), f32[8,592,128]{2,1,0:T(8,128)S(1)}, u32[]{:S(2)}, u32[]{:S(2)}) async-start(f32[8,592,128]{2,1,0:T(8,128)} %copy-done.4), calls=%async_computation.1 | async-start | bytes 4849664 | tf_op jit(solution)/shard_map/all_to_all | solution.py:48
  54.8 0.7 collective-permute-start.3
  87.3 11.0 %copy-start = (f32[8,592,128]{2,1,0:T(8,128)}, f32[8,592,128]{2,1,0:T(8,128)S(1)}, u32[]{:S(2)}) copy-start(f32[8,592,128]{2,1,0:T(8,128)S(1)} %all-to-all-done.1.mine_ref.p_ref.v_ref) | copy-start | bytes 7274500
  87.3 12.3 %collective-permute-start.4 = (f32[8,592,128]{2,1,0:T(8,128)S(1)}, f32[8,592,128]{2,1,0:T(8,128)}, u32[]{:S(2)}, u32[]{:S(2)}) collective-permute-start(f32[8,592,128]{2,1,0:T(8,128)S(1)} %all-to-all-done.1.mine_ref.p_ref.v_ref), channel_id=1, source_target_pairs={{0,8},{8,0},{16,24},{24,16},{32,40},{40,32},{48,56},{56,48},{64,72... | collective-permute-start | bytes 7274504 | tf_op jit(solution)/shard_map/ppermute | solution.py:40
  91.7 1.1 copy-start.1
  92.8 5.5 %copy-start.9 = (f32[128,128]{1,0:T(8,128)S(1)}, f32[128,128]{1,0:T(8,128)}, u32[]{:S(2)}) copy-start(f32[128,128]{1,0:T(8,128)} %param.8) | copy-start | bytes 196612
  92.8 5.8 %copy-start.8 = (f32[128,128]{1,0:T(8,128)S(1)}, f32[128,128]{1,0:T(8,128)}, u32[]{:S(2)}) copy-start(f32[128,128]{1,0:T(8,128)} %param.10) | copy-start | bytes 196612
  92.8 25.4 %all-to-all-start.2 = ((f32[8,160,256]{2,1,0:T(8,128)}), f32[8,160,256]{2,1,0:T(8,128)}, u32[]{:S(2)}, u32[]{:S(2)}) async-start(f32[8,160,256]{2,1,0:T(8,128)} %copy-done.1), calls=%async_computation.2 | async-start | bytes 2621440 | tf_op jit(solution)/shard_map/all_to_all | solution.py:48
  119.2 2.3 %collective-permute-start.5 = (f32[32,256]{1,0:T(8,128)S(1)}, f32[32,256]{1,0:T(8,128)S(1)}, u32[]{:S(2)}, u32[]{:S(2)}) collective-permute-start(f32[32,256]{1,0:T(8,128)S(1)} %slice_reduce_fusion), channel_id=1, source_target_pairs={{0,8},{8,0},{16,24},{24,16},{32,40},{40,32},{48,56},{56,48},{64,72... | collective-permute-start | bytes 98312 | tf_op jit(solution)/shard_map/ppermute | solution.py:40
  122.3 10.9 %all-to-all-start.3 = ((f32[8,32,256]{2,1,0:T(8,128)}), f32[8,32,256]{2,1,0:T(8,128)S(1)}, u32[]{:S(2)}, u32[]{:S(2)}) async-start(f32[8,32,256]{2,1,0:T(8,128)} %broadcast_in_dim.11), calls=%async_computation.3 | async-start | bytes 524288 | tf_op jit(solution)/shard_map/all_to_all | solution.py:48
  133.2 0.7 copy-start.7
